TPU v7x, 512 devices: a whole 4x8x8 slice. The times are simulated.
512 devices in a mesh: tm: 64 (over y_hi, z, core), lat: 8 (over x, y_lo).
Axes of the slice: x: 4, y: 8 (y_hi: 4, y_lo: 2; y = y_hi * 2 + y_lo), z: 8, core: 2. Of those that a mesh axis runs over, the one named last changes fastest.
Arguments:
- states: float32 [64, 3, 512, 256], P('tm', None, 'lat'), may hold values from -0.75 to 0.75
- initial_state: float32 [3, 512, 256], P(None, 'lat'), may hold values from -0.75 to 0.75
- coarse_decay: float32 [512, 256], P('lat'), may hold values from 0.015625 to 2
Outputs:
- corrected: float32 [64, 3, 512, 256], P('tm', None, 'lat')
- residual: float32 [64, 3, 512, 256], P('tm', None, 'lat')
All inputs are finite; a program needn't handle non-finite values.
Results may differ from a plain program's by a relative error of at most 0.000028.
Values sent between devices are 32-bit elements; how exact they have to be, the bound alone decides.
No kernel may reach another device: no remote copies, remote signals or barrier semaphores. Data moves between devices by JAX's collectives and lax.ppermute only.
A program may use at most 128 MiB of HBM per device.

v0:
```python
import jax
import jax.numpy as jnp
from jax import lax
from jax.sharding import PartitionSpec as P

STEPS = 4


TIME_STEP = 0.25
GRAVITY = 1.0
CORIOLIS = 0.3
MEAN_DEPTH = 1.0
TURN_ANGLE = 1.2


def extended(block, sides, width):
    for axis, dim in sides:
        count = lax.axis_size(axis)
        forward = [(i, i + 1) for i in range(count - 1)]
        forward.append((count - 1, 0))
        backward = [(target, source) for source, target in forward]
        low = lax.ppermute(
            lax.slice_in_dim(block, block.shape[dim] - width, None, axis=dim), axis, forward
        )
        high = lax.ppermute(lax.slice_in_dim(block, 0, width, axis=dim), axis, backward)
        block = jnp.concatenate([low, block, high], axis=dim)
    return block


def passed_along(x, axis, by):
    count = lax.axis_size(axis)
    pairs = [(i, i + by) for i in range(count) if 0 <= i + by < count]
    return lax.ppermute(x, axis, pairs)


def entering(value, axis, join, neutral):
    count, mine = (lax.axis_size(axis), lax.axis_index(axis))
    pieces = jax.tree.map(lambda part: lax.all_gather(part, axis), value)
    so_far = jax.tree.map(
        lambda part, zero: jnp.full_like(part, 0) + jnp.asarray(zero, part.dtype), value, neutral
    )

    def lap(position, so_far):
        longer = join(so_far, jax.tree.map(lambda part: part[position], pieces))
        return jax.tree.map(lambda new, old: jnp.where(position < mine, new, old), longer, so_far)

    return lax.fori_loop(0, count - 1, lap, so_far)


def tendency(middle, upper, lower):
    east_side = jnp.roll(middle, -1, axis=2)
    west_side = jnp.roll(middle, 1, axis=2)
    average = (east_side + west_side + upper + lower) * 0.25
    zonal = middle[1]
    meridional = middle[2]
    mass_flux = 0.5 * (
        (MEAN_DEPTH + east_side[0]) * east_side[1] - (MEAN_DEPTH + west_side[0]) * west_side[1]
    )
    mass_flux = mass_flux + 0.5 * (
        (MEAN_DEPTH + upper[0]) * upper[2] - (MEAN_DEPTH + lower[0]) * lower[2]
    )
    height_dx = 0.5 * (east_side[0] - west_side[0])
    height_dy = 0.5 * (upper[0] - lower[0])
    zonal_dx = 0.5 * (east_side[1] - west_side[1])
    zonal_dy = 0.5 * (upper[1] - lower[1])
    merid_dx = 0.5 * (east_side[2] - west_side[2])
    merid_dy = 0.5 * (upper[2] - lower[2])
    new_height = average[0] - TIME_STEP * mass_flux
    new_zonal = average[1] - TIME_STEP * (
        zonal * zonal_dx + meridional * zonal_dy + GRAVITY * height_dx - CORIOLIS * meridional
    )
    new_merid = average[2] - TIME_STEP * (
        zonal * merid_dx + meridional * merid_dy + GRAVITY * height_dy + CORIOLIS * zonal
    )
    return jnp.stack([new_height, new_zonal, new_merid], axis=0)


def step_padded(padded):
    return tendency(padded[:, 1:-1], padded[:, 2:], padded[:, :-2])


def advance(state_now):
    for _ in range(STEPS):
        state_now = step_padded(extended(state_now, (("lat", 1),), 1))
    return state_now


def apply_coarse(state_now, real_part, imag_part, height_part):
    height = state_now[0] * height_part
    zonal = real_part * state_now[1] + imag_part * state_now[2]
    merid = real_part * state_now[2] - imag_part * state_now[1]
    return jnp.stack([height, zonal, merid], axis=0)


def on_device(states, initial_state, coarse_decay):
    current = states[0]
    at_start = lax.axis_index("tm") == 0

    def previous(state_now):
        arrived = passed_along(state_now, "tm", 1)
        return jnp.where(at_start, initial_state, arrived)

    relaxed = advance(previous(current))
    before = previous(relaxed)
    ahead = advance(before)
    residual = ahead - relaxed
    shrink = jnp.exp(-coarse_decay)
    real_part = shrink * jnp.cos(jnp.float32(TURN_ANGLE))
    imag_part = shrink * jnp.sin(jnp.float32(TURN_ANGLE))
    forcing = ahead - apply_coarse(before, real_part, imag_part, shrink)

    def compose(earlier, later):
        new_real = later[0] * earlier[0] - later[1] * earlier[1]
        new_imag = later[0] * earlier[1] + later[1] * earlier[0]
        new_height = later[2] * earlier[2]
        new_term = apply_coarse(earlier[3], later[0], later[1], later[2]) + later[3]
        return (new_real, new_imag, new_height, new_term)

    ones_plane = jnp.ones_like(shrink)
    zero_plane = jnp.zeros_like(shrink)
    prefix = entering(
        (real_part, imag_part, shrink, forcing),
        "tm",
        compose,
        (ones_plane, zero_plane, ones_plane, jnp.zeros_like(forcing)),
    )
    start_state = apply_coarse(initial_state, prefix[0], prefix[1], prefix[2]) + prefix[3]
    corrected = apply_coarse(start_state, real_part, imag_part, shrink) + forcing
    return (corrected[None], residual[None])


def solution(mesh):
    placed = (P("tm", None, "lat", None), P(None, "lat", None), P("lat", None))
    return jax.shard_map(
        on_device,
        mesh=mesh,
        in_specs=placed,
        out_specs=(P("tm", None, "lat", None), P("tm", None, "lat", None)),
        check_vma=False,
    )
```

profile of v0, /device:TPU:1, one launch (start us, length us, event | category | flops | bytes accessed | tf_op | source)
XLA Modules:
  0.0 650.8 jit_solution(8330521636932778526)
XLA Ops:
  7.2 5.4 collective-permute-start
  12.6 3.9 collective-permute-done
  16.7 4.4 collective-permute-start.1
  21.1 1.9 collective-permute-start.2
  23.1 4.4 collective-permute-done.2
  28.2 1.9 collective-permute-start.3
  30.1 3.4 collective-permute-start.4
  33.6 3.0 collective-permute-done.4
  37.1 1.9 collective-permute-start.5
  39.1 3.4 collective-permute-start.6
  42.7 2.9 collective-permute-done.6
  46.2 1.9 collective-permute-start.7
  48.1 3.4 collective-permute-start.8
  51.6 3.0 collective-permute-done.8
  55.1 9.2 %collective-permute-start.9 = (f32[3,64,256]{2,1,0:T(8,128)S(1)}, f32[3,64,256]{2,1,0:T(8,128)S(1)}, u32[]{:S(2)}, u32[]{:S(2)}) collective-permute-start(f32[3,64,256]{2,1,0:T(8,128)S(1)} %pad_maximum_fusion.25), channel_id=1, source_target_pairs={{0,8},{8,16},{16,24},{24,32},{32,40},{40,48},{48,56},{56,64},{64,7... | collective-permute-start | bytes 589832 | tf_op jit(solution)/shard_map/ppermute | solution.py:33
  64.3 2.6 collective-permute-done.9
  69.2 1.9 collective-permute-start.10
  71.1 3.4 collective-permute-start.11
  74.7 2.9 collective-permute-done.11
  78.1 1.9 collective-permute-start.12
  80.1 3.4 collective-permute-start.13
  83.7 2.8 collective-permute-done.13
  87.0 1.9 collective-permute-start.14
  89.0 3.4 collective-permute-start.15
  92.6 3.2 collective-permute-done.15
  98.3 3.4 collective-permute-start.17
  101.9 2.9 collective-permute-done.17
  106.1 56.0 %all-gather.10.cloned.1.call-done = f32[4096,256]{1,0:T(8,128)} async-done(((f32[64,256]{1,0:T(8,128)}), f32[4096,256]{1,0:T(8,128)}) %all-gather.10.cloned.1.call-update) | async-done | bytes 4194320 | tf_op jit(solution)/shard_map/all_gather | solution.py:38
  162.1 86.7 %all-gather.12.cloned.1.call-done = f32[4096,256]{1,0:T(8,128)} async-done(((f32[64,256]{1,0:T(8,128)}), f32[4096,256]{1,0:T(8,128)}) %all-gather.12.cloned.1.call-update) | async-done | bytes 4194320 | tf_op jit(solution)/shard_map/all_gather | solution.py:38
  248.8 86.7 %all-gather.14.cloned.1.call-done = f32[4096,256]{1,0:T(8,128)} async-done(((f32[64,256]{1,0:T(8,128)}), f32[4096,256]{1,0:T(8,128)}) %all-gather.14.cloned.1.call-update) | async-done | bytes 4194320 | tf_op jit(solution)/shard_map/all_gather | solution.py:38
  335.5 121.2 %all-gather.8.cloned.1.call-done = f32[64,3,64,256]{3,2,1,0:T(8,128)} async-done(((f32[1,3,64,256]{3,2,1,0:T(8,128)}), f32[64,3,64,256]{3,2,1,0:T(8,128)}) %all-gather.8.cloned.1.call-update) | async-done | bytes 12582928 | tf_op jit(solution)/shard_map/all_gather | solution.py:38
  456.8 186.7 %while.20 = (s32[]{:T(128)}, f32[64,256]{1,0:T(8,128)S(1)}, f32[64,256]{1,0:T(8,128)S(1)}, f32[64,256]{1,0:T(8,128)S(1)}, f32[3,64,256]{2,1,0:T(8,128)S(1)}, /*i...) while((s32[]{:T(128)}, f32[64,256]{1,0:T(8,128)S(1)}, ...), condition=%wide.region_1.2_spmd.clone, body=%wide.region_0.1_spmd.clone.sunk | while | flops 622596 | bytes 2359448 | solution.py:47
  (350 shorter events, 195.8 us)
Async XLA Ops:
  7.2 154.9 %all-gather.10.cloned.1.call-start = ((), (), s32[]{:S(2)}) async-start(), calls=%async_computation.1 | async-start | bytes 4259840 | tf_op jit(solution)/shard_map/all_gather | solution.py:38
  7.2 9.3 %collective-permute-start = (f32[3,64,256]{2,1,0:T(8,128)}, f32[3,64,256]{2,1,0:T(8,128)S(1)}, u32[]{:S(2)}, u32[]{:S(2)}) collective-permute-start(f32[3,64,256]{2,1,0:T(8,128)} %bitcast.129), channel_id=1, source_target_pairs={{0,8},{8,16},{16,24},{24,32},{32,40},{40,48},{48,56},{56,64},{64,7... | collective-permute-start | bytes 589832 | tf_op jit(solution)/shard_map/ppermute | solution.py:33
  16.7 6.4 collective-permute-start.1
  21.1 6.5 collective-permute-start.2
  28.2 5.4 collective-permute-start.3
  30.1 6.5 collective-permute-start.4
  37.1 5.5 collective-permute-start.5
  39.1 6.5 collective-permute-start.6
  45.7 21.2 %copy-start = (f32[3,64,256]{2,1,0:T(8,128)S(1)}, f32[3,64,256]{2,1,0:T(8,128)}, u32[]{:S(2)}) copy-start(f32[3,64,256]{2,1,0:T(8,128)} %param.6) | copy-start | bytes 589828
  45.9 21.1 %copy-start.2 = (f32[64,256]{1,0:T(8,128)S(1)}, f32[64,256]{1,0:T(8,128)}, u32[]{:S(2)}) copy-start(f32[64,256]{1,0:T(8,128)} %param.7) | copy-start | bytes 196612
  46.2 5.4 collective-permute-start.7
  48.1 6.5 collective-permute-start.8
  55.1 11.8 %collective-permute-start.9 = (f32[3,64,256]{2,1,0:T(8,128)S(1)}, f32[3,64,256]{2,1,0:T(8,128)S(1)}, u32[]{:S(2)}, u32[]{:S(2)}) collective-permute-start(f32[3,64,256]{2,1,0:T(8,128)S(1)} %pad_maximum_fusion.25), channel_id=1, source_target_pairs={{0,8},{8,16},{16,24},{24,32},{32,40},{40,48},{48,56},{56,64},{64,7... | collective-permute-start | bytes 589832 | tf_op jit(solution)/shard_map/ppermute | solution.py:33
  67.6 181.1 %all-gather.12.cloned.1.call-start = ((), (), s32[]{:S(2)}) async-start(), calls=%async_computation.2 | async-start | bytes 4259840 | tf_op jit(solution)/shard_map/all_gather | solution.py:38
  68.4 267.1 %all-gather.14.cloned.1.call-start = ((), (), s32[]{:S(2)}) async-start(), calls=%async_computation.3 | async-start | bytes 4259840 | tf_op jit(solution)/shard_map/all_gather | solution.py:38
  69.1 387.6 %all-gather.8.cloned.1.call-start = ((), (), s32[]{:S(2)}) async-start(), calls=%async_computation | async-start | bytes 12779520 | tf_op jit(solution)/shard_map/all_gather | solution.py:38
  69.2 5.5 collective-permute-start.10
  71.1 6.5 collective-permute-start.11
  78.1 5.5 collective-permute-start.12
  80.1 6.5 collective-permute-start.13
  87.0 5.5 collective-permute-start.14
  89.0 6.8 %collective-permute-start.15 = (f32[3,1,256]{2,1,0:T(1,128)S(1)}, f32[3,1,256]{2,1,0:T(1,128)S(1)}, u32[]{:S(2)}, u32[]{:S(2)}) collective-permute-start(f32[3,1,256]{2,1,0:T(1,128)S(1)} %get-tuple-element.275), channel_id=1, source_target_pairs={{0,1},{1,2},{2,3},{3,4},{4,5},{5,6},{6,7},{7,0},{8,9},{9,10},{10,1... | collective-permute-start | bytes 9224 | tf_op jit(solution)/shard_map/ppermute | solution.py:22
  96.3 5.5 collective-permute-start.16
  98.3 6.5 collective-permute-start.17
  456.8 186.8 %copy-start.1 = (f32[1,3,64,256]{3,2,1,0:T(8,128)S(1)}, f32[1,3,64,256]{3,2,1,0:T(8,128)}, u32[]{:S(2)}) copy-start(f32[1,3,64,256]{3,2,1,0:T(8,128)} %get-tuple-element.258) | copy-start | bytes 589828
Sparse Core Ops, SparseCore 0:
  67.8 94.2 all-gather.9
  165.4 83.3 all-gather.11
  252.2 83.3 all-gather.13
  339.3 117.4 all-gather.7
where the time goes:
time: 659 us; the launch traced here: 651 us
  waiting for transfers between devices  384 us (58%)
  other arithmetic  191 us (29%)
  starting transfers between devices  58 us (9%)
  between operations  14.5 us (2%)
    all_gather x4, waiting for transfers between devices, entering(): pieces = jax.tree.map(lambda part: lax.all_gather(part, axis), value)  351 us
    select_n x126, other arithmetic, lap(): jnp.where(position < mine, new, old)  124 us
    add x63, other arithmetic, apply_coarse(): zonal = real_part * state_now[1] + imag_part * state_now[2]  59.3 us
    ppermute x8, starting transfers between devices, extended(): lax.ppermute(lax.slice_in_dim(block, block.shape[dim] - width, None, axis...  25.5 us
    ppermute x8, waiting for transfers between devices, extended(): lax.ppermute(lax.slice_in_dim(block, block.shape[dim] - width, None, axis...  25 us
    ppermute x8, starting transfers between devices, extended(): lax.ppermute(lax.slice_in_dim(block, 0, width, axis=dim), axis, backward)  17.8 us
    ppermute x2, starting transfers between devices, passed_along(): return lax.ppermute(x, axis, pairs)  14.6 us
  transfers between devices with their start and end apart: 22, of which 14 were waited for; matrix products, arithmetic and copies ran while one was open for 1% of the time, Pallas kernels for 0%

commit v1 on v0

v1 whole, which is shorter than its diff:
```python
import functools

import jax
import jax.numpy as jnp
import numpy as np
from jax import lax
from jax.experimental import pallas as pl
from jax.experimental.pallas import tpu as pltpu
from jax.sharding import PartitionSpec as P

STEPS = 4
TIME_STEP = 0.25
CORIOLIS = 0.3
TURN_ANGLE = 1.2
LANES = 128
HALO = 2 * STEPS


def turns(blocks):
    turn = complex(np.cos(np.float32(TURN_ANGLE)), np.sin(np.float32(TURN_ANGLE)))
    powers = np.cumprod(np.full(blocks, turn, np.complex128))
    return np.repeat(np.concatenate([powers.real, powers.imag])[:, None], LANES, 1).astype(np.float32)


def fine_step(height, zonal, merid):
    rows = height.shape[0]
    lons = height.shape[1]

    def sides(a):
        return (
            pltpu.roll(a, lons - 1, 1),
            pltpu.roll(a, 1, 1),
            pltpu.roll(a, rows - 1, 0),
            pltpu.roll(a, 1, 0),
        )

    he, hw, hn, hs = sides(height)
    ze, zw, zn, zs = sides(zonal)
    me, mw, mn, ms = sides(merid)
    half = 0.5 * TIME_STEP
    flux = ((1.0 + he) * ze - (1.0 + hw) * zw) + ((1.0 + hn) * mn - (1.0 + hs) * ms)
    new_height = 0.25 * ((he + hw) + (hn + hs)) - half * flux
    new_zonal = (
        0.25 * ((ze + zw) + (zn + zs))
        - half * (zonal * (ze - zw) + merid * (zn - zs) + (he - hw))
        + (TIME_STEP * CORIOLIS) * merid
    )
    new_merid = (
        0.25 * ((me + mw) + (mn + ms))
        - half * (zonal * (me - mw) + merid * (mn - ms) + (hn - hs))
        - (TIME_STEP * CORIOLIS) * zonal
    )
    return new_height, new_zonal, new_merid


def turn_of(turn_ref, slot):
    blocks = turn_ref.shape[0] // 2
    return turn_ref[pl.ds(slot, 1)], turn_ref[pl.ds(slot + blocks, 1)]


def two_blocks(state):
    for _ in range(STEPS):
        state = fine_step(*state)
    relaxed = state
    for _ in range(STEPS):
        state = fine_step(*state)
    return relaxed, state


def forcing(turn_ref, decay, relaxed, ahead):
    blocks = turn_ref.shape[0] // 2
    mine = lax.axis_index("tm")
    shrink = jnp.where(mine == blocks - 1, 0.0, jnp.exp(-decay))
    cos1, sin1 = turn_of(turn_ref, 0)
    cos, sin = turn_of(turn_ref, lax.rem(mine + 2, blocks))
    height = ahead[0] - shrink * relaxed[0]
    zonal = ahead[1] - shrink * (cos1 * relaxed[1] + sin1 * relaxed[2])
    merid = ahead[2] - shrink * (cos1 * relaxed[2] - sin1 * relaxed[1])
    return height, cos * zonal - sin * merid, cos * merid + sin * zonal


def put_forcing(turn_ref, decay_ref, relaxed_ref, ahead_ref, term_ref, rows):
    lons = decay_ref.shape[1]
    per_plane = term_ref.shape[0] // 3
    for row in rows:
        for col in range(0, lons, LANES):
            where = (slice(row, row + 8), slice(col, col + LANES))
            relaxed = [relaxed_ref[(plane, *where)] for plane in range(3)]
            ahead = [ahead_ref[(plane, *where)] for plane in range(3)]
            at = row * lons // LANES + col * 8 // LANES
            for plane, term in enumerate(forcing(turn_ref, decay_ref[where], relaxed, ahead)):
                to = plane * per_plane + at
                term_ref[to : to + 8] = term


def inner_kernel(turn_ref, state_ref, decay_ref, term_ref, relaxed_ref, ahead_ref, term, sem):
    rows = state_ref.shape[1]
    relaxed, ahead = two_blocks([state_ref[plane] for plane in range(3)])
    for plane in range(3):
        relaxed_ref[plane] = relaxed[plane]
        ahead_ref[plane] = ahead[plane]
    put_forcing(turn_ref, decay_ref, relaxed_ref, ahead_ref, term, range(8, rows - 8, 8))
    edge = 8 * decay_ref.shape[1] // LANES
    per_plane = term.shape[0] // 3
    copies = []
    for plane in range(3):
        part = pl.ds(plane * per_plane + edge, per_plane - 2 * edge)
        copies.append(pltpu.make_async_copy(term.at[part], term_ref.at[part], sem.at[plane]))
        copies[-1].start()
    for copy in copies:
        copy.wait()


def edge_kernel(
    turn_ref, state_ref, first_ref, second_ref, decay_ref, term_in, relaxed_in, ahead_in,
    term_ref, relaxed_ref, ahead_ref, term, sem,
):
    even = lax.rem(lax.axis_index("lat"), 2) == 0
    rows = state_ref.shape[1]
    state = []
    for plane in range(3):
        first, second = first_ref[plane], second_ref[plane]
        below = jnp.where(even, second, first)
        above = jnp.where(even, first, second)
        low, high = state_ref[plane, : 2 * HALO], state_ref[plane, rows - 2 * HALO :]
        state.append(jnp.concatenate([below, low, high, above], axis=0))
    relaxed, ahead = two_blocks(state)
    for plane in range(3):
        for to, inner, value in (
            (relaxed_ref, relaxed_in, relaxed[plane]),
            (ahead_ref, ahead_in, ahead[plane]),
        ):
            to[plane, HALO : rows - HALO] = inner[plane, HALO : rows - HALO]
            to[plane, :HALO] = value[HALO : 2 * HALO]
            to[plane, rows - HALO :] = value[4 * HALO : 5 * HALO]
    put_forcing(turn_ref, decay_ref, relaxed_ref, ahead_ref, term, (0, rows - 8))
    edge = 8 * decay_ref.shape[1] // LANES
    per_plane = term.shape[0] // 3
    ends = [0, *(plane * per_plane for plane in (1, 2)), 3 * per_plane]
    copies = []
    for k, end in enumerate(ends):
        start, stop = max(end - edge, 0), min(end + edge, 3 * per_plane)
        part = pl.ds(start, stop - start)
        copies.append(pltpu.make_async_copy(term.at[part], term_ref.at[part], sem.at[k]))
        copies[-1].start()
    for copy in copies:
        copy.wait()


def solve_kernel(blocks, decay_ref, term_ref, value_ref, values, sem):
    shrink = jnp.exp(-decay_ref[...])
    each = shrink.shape[0]
    parts = sem.shape[0]

    def at(slot):
        return slice(slot * each, (slot + 1) * each)

    value = term_ref[at(blocks - 1)]
    copies = []
    for slot in range(blocks):
        if slot >= 2:
            value = shrink * value + term_ref[at(slot - 2)]
        values[at(slot)] = value
        if (slot + 1) % (blocks // parts) == 0:
            size = each * blocks // parts
            part = pl.ds(len(copies) * size, size)
            copies.append(pltpu.make_async_copy(values.at[part], value_ref.at[part], sem.at[len(copies)]))
            copies[-1].start()
    for copy in copies:
        copy.wait()


def residual_kernel(relaxed_ref, ahead_ref, residual_ref):
    first = lax.axis_index("tm") == 0
    for plane in range(3):
        relaxed = relaxed_ref[plane]
        residual_ref[0, plane] = jnp.where(first, relaxed, ahead_ref[plane]) - relaxed


def finish_kernel(turn_ref, value_ref, relaxed_ref, corrected_ref):
    mine = lax.axis_index("tm")
    first = mine == 0
    cos, sin = turn_of(turn_ref, mine)
    rows, lons = corrected_ref.shape[2:]
    per_plane = rows * lons // LANES
    at = 0
    for row in range(0, rows, 8):
        for col in range(0, lons, LANES):
            height, zonal, merid = (
                value_ref[plane * per_plane + at : plane * per_plane + at + 8] for plane in range(3)
            )
            values = (height, cos * zonal + sin * merid, cos * merid - sin * zonal)
            for plane in range(3):
                block = (plane, slice(row, row + 8), slice(col, col + LANES))
                corrected_ref[(0, *block)] = jnp.where(first, relaxed_ref[block], values[plane])
            at += 8


def on_device(states, initial_state, coarse_decay):
    blocks, slabs = lax.axis_size("tm"), lax.axis_size("lat")
    mine, slab = lax.axis_index("tm"), lax.axis_index("lat")
    _, planes, rows, lons = states.shape
    size = planes * rows * lons
    each = size // LANES // blocks
    vmem = pl.BlockSpec(memory_space=pltpu.VMEM)
    hbm = pl.BlockSpec(memory_space=pltpu.HBM)
    f32 = functools.partial(jax.ShapeDtypeStruct, dtype=jnp.float32)
    whole, flat = f32((planes, rows, lons)), f32((size // LANES, LANES))
    params = pltpu.CompilerParams(vmem_limit_bytes=32 << 20)
    turn = jnp.asarray(turns(blocks))

    def long(steps):
        return pl.CostEstimate(flops=steps * size, bytes_accessed=8 * size, transcendentals=0)

    state = jnp.where(mine == blocks - 1, initial_state, states[0])
    even = slab % 2 == 0
    low, high = state[:, :HALO], state[:, -HALO:]
    inner = [(i, i ^ 1) for i in range(slabs)]
    outer = [(i, (i - 1 if i % 2 == 0 else i + 1) % slabs) for i in range(slabs)]
    first = lax.ppermute(jnp.where(even, high, low), "lat", inner)
    second = lax.ppermute(jnp.where(even, low, high), "lat", outer)

    tiles = coarse_decay.reshape(rows // 8, 8, lons // LANES, LANES).transpose(0, 2, 1, 3)
    tiles = tiles.reshape(-1, LANES)
    tiles = jnp.concatenate([tiles, tiles[:each]], axis=0)
    own_decay = lax.dynamic_slice_in_dim(tiles, lax.rem(mine * each, rows * lons // LANES), each, 0)

    term, relaxed, ahead = pl.pallas_call(
        inner_kernel,
        out_shape=(flat, whole, whole),
        in_specs=[vmem] * 3,
        out_specs=(hbm, vmem, vmem),
        scratch_shapes=[pltpu.VMEM(flat.shape, jnp.float32), pltpu.SemaphoreType.DMA((3,))],
        compiler_params=params,
        cost_estimate=long(10**3),
    )(turn, state, coarse_decay)
    term, relaxed, ahead = pl.pallas_call(
        edge_kernel,
        out_shape=(flat, whole, whole),
        in_specs=[vmem] * 5 + [hbm, vmem, vmem],
        out_specs=(hbm, vmem, vmem),
        scratch_shapes=[pltpu.VMEM(flat.shape, jnp.float32), pltpu.SemaphoreType.DMA((4,))],
        input_output_aliases={5: 0},
        compiler_params=params,
    )(turn, state, first, second, coarse_decay, term, relaxed, ahead)

    def shifted(x, by):
        return lax.ppermute(x, "tm", [(i, (i + by) % blocks) for i in range(blocks)])

    relaxed, ahead = shifted(relaxed, 1), shifted(ahead, 2)
    residual = pl.pallas_call(
        residual_kernel,
        out_shape=f32((1, planes, rows, lons)),
        in_specs=[vmem, vmem],
        out_specs=vmem,
        compiler_params=params,
        cost_estimate=long(10**6),
    )(relaxed, ahead)
    term = lax.all_to_all(term.reshape(blocks, -1), "tm", 0, 0, tiled=True)
    value = pl.pallas_call(
        functools.partial(solve_kernel, blocks),
        out_shape=flat,
        in_specs=[vmem, vmem],
        out_specs=hbm,
        scratch_shapes=[pltpu.VMEM(flat.shape, jnp.float32), pltpu.SemaphoreType.DMA((4,))],
        compiler_params=params,
    )(own_decay, term.reshape(-1, LANES))
    value = lax.all_to_all(value.reshape(blocks, -1), "tm", 0, 0, tiled=True)
    corrected = pl.pallas_call(
        finish_kernel,
        out_shape=f32((1, planes, rows, lons)),
        in_specs=[vmem] * 3,
        out_specs=vmem,
        compiler_params=params,
    )(turn, value.reshape(-1, LANES), relaxed)
    return (corrected, residual)


def solution(mesh):
    placed = (P("tm", None, "lat", None), P(None, "lat", None), P("lat", None))
    return jax.shard_map(
        on_device,
        mesh=mesh,
        in_specs=placed,
        out_specs=(P("tm", None, "lat", None), P("tm", None, "lat", None)),
        check_vma=False,
    )
```

time: 659 us -> 64.8 us (0.10); the launches traced: 651 us -> 64.4 us
  waiting for transfers between devices: 384 us -> 18.9 us
  other arithmetic: 191 us -> 1.02 us
  starting transfers between devices: 58 us -> 37.5 us
  between operations: 14.5 us -> 0.81 us
    all_gather x4 -> x0, waiting for transfers between devices: 351 us -> none  [entering(): pieces = jax.tree.map(lambda part: lax.all_gather(part, axis), value)]
    select_n x128 -> x2, other arithmetic: 124 us -> 1 us  [the longest x1 0.99 us: on_device(): state = jnp.where(mine == blocks - 1, initial_state, states[0])]
    add x65 -> x0, other arithmetic: 60 us -> none  [the longest x63 59.3 us: apply_coarse(): zonal = real_part * state_now[1] + imag_part * state_now[2]]
    ppermute x18 -> x4, starting transfers between devices: 57.9 us -> 14.9 us  [the longest x2 6.63 us: shifted(): lax.ppermute(x, 'tm', [(i, (i + by) % blocks) for i in range(blocks)])]
    ppermute x18 -> x4, waiting for transfers between devices: 31.5 us -> 1.86 us  [the longest x2 1.63 us: shifted(): lax.ppermute(x, 'tm', [(i, (i + by) % blocks) for i in range(blocks)])]
    all_to_all x0 -> x2, starting transfers between devices: none -> 22.6 us  [the longest x1 17.3 us: on_device(): term = lax.all_to_all(term.reshape(blocks, -1), 'tm', 0, 0, tiled=True)]
    all_to_all x0 -> x2, waiting for transfers between devices: none -> 17.1 us  [the longest x1 10.6 us: on_device(): value = lax.all_to_all(value.reshape(blocks, -1), 'tm', 0, 0, tiled=True)]
  transfers between devices with their start and end apart: 22 -> 6, of which waited for: 14 -> 4; matrix products, arithmetic and copies ran while one was open for 1% -> 0% of each run, Pallas kernels for 0% -> 6%
where the time goes in v1:
time: 64.8 us; the launch traced here: 64.4 us
  starting transfers between devices  37.5 us (58%)
  waiting for transfers between devices  18.9 us (29%)
  Pallas kernels  6.1 us (9%)
  other arithmetic  1.02 us (2%)
  between operations  0.81 us (1%)
    all_to_all x1, starting transfers between devices, on_device(): term = lax.all_to_all(term.reshape(blocks, -1), 'tm', 0, 0, tiled=True)  17.3 us
    all_to_all x1, waiting for transfers between devices, on_device(): value = lax.all_to_all(value.reshape(blocks, -1), 'tm', 0, 0, tiled=True)  10.6 us
    ppermute x2, starting transfers between devices, shifted(): lax.ppermute(x, 'tm', [(i, (i + by) % blocks) for i in range(blocks)])  6.63 us
    all_to_all x1, waiting for transfers between devices, on_device(): term = lax.all_to_all(term.reshape(blocks, -1), 'tm', 0, 0, tiled=True)  6.47 us
    all_to_all x1, starting transfers between devices, on_device(): value = lax.all_to_all(value.reshape(blocks, -1), 'tm', 0, 0, tiled=True)  5.22 us
    ppermute x1, starting transfers between devices, on_device(): second = lax.ppermute(jnp.where(even, low, high), 'lat', outer)  4.27 us
    ppermute x1, starting transfers between devices, on_device(): first = lax.ppermute(jnp.where(even, high, low), 'lat', inner)  4.03 us
    pallas_call x1, Pallas kernels, on_device(): pl.pallas_call(inner_kernel, out_shape=(flat, whole, whole), in_specs=[vm...  2.13 us
  transfers between devices with their start and end apart: 6, of which 4 were waited for; matrix products, arithmetic and copies ran while one was open for 0% of the time, Pallas kernels for 6%

profile of v1, /device:TPU:1, one launch (start us, length us, event | category | flops | bytes accessed | tf_op | source)
XLA Modules:
  0.0 64.4 jit_solution(7686342127772700668)
XLA Ops:
  0.6 0.0 copy-start.1
  0.7 1.0 %bitcast_select_fusion.state_ref = f32[3,64,256]{2,1,0:T(8,128)S(1)} fusion(f32[3,64,256]{2,1,0:T(8,128)} %param.5, f32[1,3,64,256]{3,2,1,0:T(8,128)} %param.4, pred[]{:T(512)S(6)} %eq.8), kind=kLoop, calls=%fused_computation | loop fusion | flops 49152 | bytes 589825 | tf_op jit(solution)/shard_map/jit(_where)/select_n | solution.py:215
  1.7 0.0 copy-start
  1.7 4.0 %collective-permute-start = (f32[3,8,256]{2,1,0:T(8,128)S(1)}, f32[3,8,256]{2,1,0:T(8,128)S(1)}, u32[]{:S(2)}, u32[]{:S(2)}) collective-permute-start(f32[3,8,256]{2,1,0:T(8,128)S(1)} %get-tuple-element.15), channel_id=1, source_target_pairs={{0,1},{1,0},{2,3},{3,2},{4,5},{5,4},{6,7},{7,6},{8,9},{9,8},{10,11... | collective-permute-start | bytes 73736 | tf_op jit(solution)/shard_map/ppermute | solution.py:220
  5.7 4.3 %collective-permute-start.1 = (f32[3,8,256]{2,1,0:T(8,128)S(1)}, f32[3,8,256]{2,1,0:T(8,128)S(1)}, u32[]{:S(2)}, u32[]{:S(2)}) collective-permute-start(f32[3,8,256]{2,1,0:T(8,128)S(1)} %get-tuple-element.14), channel_id=1, source_target_pairs={{0,7},{1,2},{2,1},{3,4},{4,3},{5,6},{6,5},{7,0},{8,15},{9,10},{10,... | collective-permute-start | bytes 73736 | tf_op jit(solution)/shard_map/ppermute | solution.py:221
  10.0 0.0 copy-done.1
  10.0 0.0 copy-done
  10.0 2.1 %shard_map.59 = (f32[384,128]{1,0:T(8,128)}, f32[3,64,256]{2,1,0:T(8,128)S(1)}, f32[3,64,256]{2,1,0:T(8,128)S(1)}) custom-call(f32[128,128]{1,0:T(8,128)S(1)} %copy-done.1, f32[3,64,256]{2,1,0:T(8,128)S(1)} %bitcast_select_fusion.state_ref, f32[64,256]{1,0:T(8,128)S(1)} %copy-done), custom_call_target="tpu_custom_call" | custom-call | flops 49152000 | bytes 393216 | tf_op jit(solution)/shard_map/pallas_call | solution.py:228
  12.2 0.0 collective-permute-done.first_ref
  12.2 0.2 collective-permute-done.1.second_ref
  12.4 1.8 %shard_map.60 = (f32[384,128]{1,0:T(8,128)}, f32[3,64,256]{2,1,0:T(8,128)S(1)}, f32[3,64,256]{2,1,0:T(8,128)S(1)}) custom-call(f32[128,128]{1,0:T(8,128)S(1)} %copy-done.1, f32[3,64,256]{2,1,0:T(8,128)S(1)} %bitcast_select_fusion.state_ref, f32[3,8,256]{2,1,0:T(8,128)S(1)} %collective-permute-done.first_ref, ...), custom_call_target="tpu_custom_call", output_to_operand_aliasing={{0}: (5, {})} | custom-call | tf_op jit(solution)/shard_map/pallas_call | solution.py:237
  14.2 17.3 %all-to-all-start = ((f32[64,1,768]{2,1,0:T(1,128)}), f32[64,1,768]{2,1,0:T(1,128)S(1)}, u32[]{:S(2)}, u32[]{:S(2)}) async-start(f32[64,1,768]{2,1,0:T(1,128)} %bitcast.6), calls=%async_computation | async-start | bytes 393216 | tf_op jit(solution)/shard_map/all_to_all | solution.py:259
  31.5 3.5 %collective-permute-start.2 = (f32[3,64,256]{2,1,0:T(8,128)S(1)}, f32[3,64,256]{2,1,0:T(8,128)S(1)}, u32[]{:S(2)}, u32[]{:S(2)}) collective-permute-start(f32[3,64,256]{2,1,0:T(8,128)S(1)} %get-tuple-element.12), channel_id=1, source_target_pairs={{0,8},{8,16},{16,24},{24,32},{32,40},{40,48},{48,56},{56,64},{64,7... | collective-permute-start | bytes 589832 | tf_op jit(solution)/shard_map/ppermute | solution.py:248
  35.1 3.1 %collective-permute-start.3 = (f32[3,64,256]{2,1,0:T(8,128)S(1)}, f32[3,64,256]{2,1,0:T(8,128)S(1)}, u32[]{:S(2)}, u32[]{:S(2)}) collective-permute-start(f32[3,64,256]{2,1,0:T(8,128)S(1)} %get-tuple-element.13), channel_id=1, source_target_pairs={{0,16},{8,24},{16,32},{24,40},{32,48},{40,56},{48,64},{56,72},{64,... | collective-permute-start | bytes 589832 | tf_op jit(solution)/shard_map/ppermute | solution.py:248
  38.2 6.5 %all-to-all-done = f32[64,1,768]{2,1,0:T(1,128)S(1)} async-done(((f32[64,1,768]{2,1,0:T(1,128)}), f32[64,1,768]{2,1,0:T(1,128)S(1)}, u32[]{:S(2)}, u32[]{:S(2)}) %all-to-all-start) | async-done | bytes 196640 | tf_op jit(solution)/shard_map/all_to_all | solution.py:259
  44.7 0.8 %shard_map.61 = f32[384,128]{1,0:T(8,128)} custom-call(f32[6,128]{1,0:T(8,128)S(1)} %fusion.decay_ref, f32[384,128]{1,0:T(8,128)S(1)} %bitcast.11), custom_call_target="tpu_custom_call" | custom-call | tf_op jit(solution)/shard_map/pallas_call | solution.py:260
  45.5 5.2 %all-to-all-start.1 = ((f32[64,1,768]{2,1,0:T(1,128)}), f32[64,1,768]{2,1,0:T(1,128)S(1)}, u32[]{:S(2)}, u32[]{:S(2)}) async-start(f32[64,1,768]{2,1,0:T(1,128)} %bitcast.8), calls=%async_computation.1 | async-start | bytes 393216 | tf_op jit(solution)/shard_map/all_to_all | solution.py:268
  50.7 0.0 collective-permute-done.2.relaxed_ref
  50.7 1.6 %collective-permute-done.3.ahead_ref = f32[3,64,256]{2,1,0:T(8,128)S(1)} collective-permute-done((f32[3,64,256]{2,1,0:T(8,128)S(1)}, f32[3,64,256]{2,1,0:T(8,128)S(1)}, u32[]{:S(2)}, u32[]{:S(2)}) %collective-permute-start.3) | collective-permute-done | bytes 196640 | tf_op jit(solution)/shard_map/ppermute | solution.py:248
  52.4 0.7 %shard_map.63 = f32[1,3,64,256]{3,2,1,0:T(8,128)} custom-call(f32[3,64,256]{2,1,0:T(8,128)S(1)} %collective-permute-done.2.relaxed_ref, f32[3,64,256]{2,1,0:T(8,128)S(1)} %collective-permute-done.3.ahead_ref), custom_call_target="tpu_custom_call" | custom-call | flops 49152000000 | bytes 393216 | tf_op jit(solution)/shard_map/pallas_call | solution.py:251
  53.1 10.6 %all-to-all-done.1 = f32[64,1,768]{2,1,0:T(1,128)S(1)} async-done(((f32[64,1,768]{2,1,0:T(1,128)}), f32[64,1,768]{2,1,0:T(1,128)S(1)}, u32[]{:S(2)}, u32[]{:S(2)}) %all-to-all-start.1) | async-done | bytes 196640 | tf_op jit(solution)/shard_map/all_to_all | solution.py:268
  63.7 0.7 %shard_map.62 = f32[1,3,64,256]{3,2,1,0:T(8,128)} custom-call(f32[128,128]{1,0:T(8,128)S(1)} %copy-done.1, f32[384,128]{1,0:T(8,128)S(1)} %bitcast.12, f32[3,64,256]{2,1,0:T(8,128)S(1)} %collective-permute-done.2.relaxed_ref), custom_call_target="tpu_custom_call" | custom-call | tf_op jit(solution)/shard_map/pallas_call | solution.py:269
  (3 shorter events, 0.0 us)
Async XLA Ops:
  0.6 9.4 %copy-start.1 = (f32[128,128]{1,0:T(8,128)S(1)}, f32[128,128]{1,0:T(8,128)}, u32[]{:S(2)}) copy-start(f32[128,128]{1,0:T(8,128)} %constant.35.clone.turn_ref) | copy-start | bytes 196612
  1.7 8.4 %copy-start = (f32[64,256]{1,0:T(8,128)S(1)}, f32[64,256]{1,0:T(8,128)}, u32[]{:S(2)}) copy-start(f32[64,256]{1,0:T(8,128)} %decay_ref.3) | copy-start | bytes 196612
  1.7 10.5 %collective-permute-start = (f32[3,8,256]{2,1,0:T(8,128)S(1)}, f32[3,8,256]{2,1,0:T(8,128)S(1)}, u32[]{:S(2)}, u32[]{:S(2)}) collective-permute-start(f32[3,8,256]{2,1,0:T(8,128)S(1)} %get-tuple-element.15), channel_id=1, source_target_pairs={{0,1},{1,0},{2,3},{3,2},{4,5},{5,4},{6,7},{7,6},{8,9},{9,8},{10,11... | collective-permute-start | bytes 73736 | tf_op jit(solution)/shard_map/ppermute | solution.py:220
  5.7 6.7 %collective-permute-start.1 = (f32[3,8,256]{2,1,0:T(8,128)S(1)}, f32[3,8,256]{2,1,0:T(8,128)S(1)}, u32[]{:S(2)}, u32[]{:S(2)}) collective-permute-start(f32[3,8,256]{2,1,0:T(8,128)S(1)} %get-tuple-element.14), channel_id=1, source_target_pairs={{0,7},{1,2},{2,1},{3,4},{4,3},{5,6},{6,5},{7,0},{8,15},{9,10},{10,... | collective-permute-start | bytes 73736 | tf_op jit(solution)/shard_map/ppermute | solution.py:221
  14.2 30.5 %all-to-all-start = ((f32[64,1,768]{2,1,0:T(1,128)}), f32[64,1,768]{2,1,0:T(1,128)S(1)}, u32[]{:S(2)}, u32[]{:S(2)}) async-start(f32[64,1,768]{2,1,0:T(1,128)} %bitcast.6), calls=%async_computation | async-start | bytes 393216 | tf_op jit(solution)/shard_map/all_to_all | solution.py:259
  31.5 19.2 %collective-permute-start.2 = (f32[3,64,256]{2,1,0:T(8,128)S(1)}, f32[3,64,256]{2,1,0:T(8,128)S(1)}, u32[]{:S(2)}, u32[]{:S(2)}) collective-permute-start(f32[3,64,256]{2,1,0:T(8,128)S(1)} %get-tuple-element.12), channel_id=1, source_target_pairs={{0,8},{8,16},{16,24},{24,32},{32,40},{40,48},{48,56},{56,64},{64,7... | collective-permute-start | bytes 589832 | tf_op jit(solution)/shard_map/ppermute | solution.py:248
  35.1 17.3 %collective-permute-start.3 = (f32[3,64,256]{2,1,0:T(8,128)S(1)}, f32[3,64,256]{2,1,0:T(8,128)S(1)}, u32[]{:S(2)}, u32[]{:S(2)}) collective-permute-start(f32[3,64,256]{2,1,0:T(8,128)S(1)} %get-tuple-element.13), channel_id=1, source_target_pairs={{0,16},{8,24},{16,32},{24,40},{32,48},{40,56},{48,64},{56,72},{64,... | collective-permute-start | bytes 589832 | tf_op jit(solution)/shard_map/ppermute | solution.py:248
  45.5 18.2 %all-to-all-start.1 = ((f32[64,1,768]{2,1,0:T(1,128)}), f32[64,1,768]{2,1,0:T(1,128)S(1)}, u32[]{:S(2)}, u32[]{:S(2)}) async-start(f32[64,1,768]{2,1,0:T(1,128)} %bitcast.8), calls=%async_computation.1 | async-start | bytes 393216 | tf_op jit(solution)/shard_map/all_to_all | solution.py:268

commit v2 on v1

--- a/solution.py
+++ b/solution.py
@@ -112,7 +112,7 @@
 
 
 def edge_kernel(
-    turn_ref, state_ref, first_ref, second_ref, decay_ref, term_in, relaxed_in, ahead_in,
+    turn_ref, state_ref, second_ref, first_ref, decay_ref, term_in, relaxed_in, ahead_in,
     term_ref, relaxed_ref, ahead_ref, term, sem,
 ):
     even = lax.rem(lax.axis_index("lat"), 2) == 0
@@ -125,17 +125,16 @@
         low, high = state_ref[plane, : 2 * HALO], state_ref[plane, rows - 2 * HALO :]
         state.append(jnp.concatenate([below, low, high, above], axis=0))
     relaxed, ahead = two_blocks(state)
-    for plane in range(3):
-        for to, inner, value in (
-            (relaxed_ref, relaxed_in, relaxed[plane]),
-            (ahead_ref, ahead_in, ahead[plane]),
-        ):
-            to[plane, HALO : rows - HALO] = inner[plane, HALO : rows - HALO]
-            to[plane, :HALO] = value[HALO : 2 * HALO]
-            to[plane, rows - HALO :] = value[4 * HALO : 5 * HALO]
-    put_forcing(turn_ref, decay_ref, relaxed_ref, ahead_ref, term, (0, rows - 8))
-    edge = 8 * decay_ref.shape[1] // LANES
+    lons = decay_ref.shape[1]
+    edge = 8 * lons // LANES
     per_plane = term.shape[0] // 3
+    for row, at in ((0, HALO), (rows - 8, 4 * HALO)):
+        for col in range(0, lons, LANES):
+            cols = slice(col, col + LANES)
+            tiles = [[a[at : at + 8, cols] for a in state] for state in (relaxed, ahead)]
+            to = row * lons // LANES + col * 8 // LANES
+            for plane, value in enumerate(forcing(turn_ref, decay_ref[row : row + 8, cols], *tiles)):
+                term[plane * per_plane + to : plane * per_plane + to + 8] = value
     ends = [0, *(plane * per_plane for plane in (1, 2)), 3 * per_plane]
     copies = []
     for k, end in enumerate(ends):
@@ -143,28 +142,37 @@
         part = pl.ds(start, stop - start)
         copies.append(pltpu.make_async_copy(term.at[part], term_ref.at[part], sem.at[k]))
         copies[-1].start()
+    for to, inner, values in ((relaxed_ref, relaxed_in, relaxed), (ahead_ref, ahead_in, ahead)):
+        for plane, value in enumerate(values):
+            to[plane, HALO : rows - HALO] = inner[plane, HALO : rows - HALO]
+            to[plane, :HALO] = value[HALO : 2 * HALO]
+            to[plane, rows - HALO :] = value[4 * HALO : 5 * HALO]
     for copy in copies:
         copy.wait()
 
 
-def solve_kernel(blocks, decay_ref, term_ref, value_ref, values, sem):
+def solve_kernel(blocks, lead, decay_ref, term_ref, value_ref, values, sem):
     shrink = jnp.exp(-decay_ref[...])
     each = shrink.shape[0]
     parts = sem.shape[0]
 
     def at(slot):
-        return slice(slot * each, (slot + 1) * each)
+        place = (slot - lead) % blocks
+        return slice(place * each, (place + 1) * each)
 
     value = term_ref[at(blocks - 1)]
-    copies = []
+    size = each * blocks // parts
+    copies, done = [], set()
     for slot in range(blocks):
         if slot >= 2:
             value = shrink * value + term_ref[at(slot - 2)]
         values[at(slot)] = value
-        if (slot + 1) % (blocks // parts) == 0:
-            size = each * blocks // parts
-            part = pl.ds(len(copies) * size, size)
-            copies.append(pltpu.make_async_copy(values.at[part], value_ref.at[part], sem.at[len(copies)]))
+        done.add((slot - lead) % blocks * parts // blocks)
+        later = {(more - lead) % blocks * parts // blocks for more in range(slot + 1, blocks)}
+        for k in sorted(done - later):
+            done.remove(k)
+            part = pl.ds(k * size, size)
+            copies.append(pltpu.make_async_copy(values.at[part], value_ref.at[part], sem.at[k]))
             copies[-1].start()
     for copy in copies:
         copy.wait()
@@ -208,6 +216,13 @@
     whole, flat = f32((planes, rows, lons)), f32((size // LANES, LANES))
     params = pltpu.CompilerParams(vmem_limit_bytes=32 << 20)
     turn = jnp.asarray(turns(blocks))
+    lead = 5 * blocks // 8
+    places = [[(place + lead) % blocks for place in range(blocks)]]
+
+    def exchanged(x):
+        return lax.all_to_all(
+            x.reshape(blocks, -1), "tm", 0, 0, axis_index_groups=places, tiled=True
+        ).reshape(-1, LANES)
 
     def long(steps):
         return pl.CostEstimate(flops=steps * size, bytes_accessed=8 * size, transcendentals=0)
@@ -217,13 +232,14 @@
     low, high = state[:, :HALO], state[:, -HALO:]
     inner = [(i, i ^ 1) for i in range(slabs)]
     outer = [(i, (i - 1 if i % 2 == 0 else i + 1) % slabs) for i in range(slabs)]
+    second = lax.ppermute(jnp.where(even, low, high), "lat", outer)
     first = lax.ppermute(jnp.where(even, high, low), "lat", inner)
-    second = lax.ppermute(jnp.where(even, low, high), "lat", outer)
 
     tiles = coarse_decay.reshape(rows // 8, 8, lons // LANES, LANES).transpose(0, 2, 1, 3)
     tiles = tiles.reshape(-1, LANES)
     tiles = jnp.concatenate([tiles, tiles[:each]], axis=0)
-    own_decay = lax.dynamic_slice_in_dim(tiles, lax.rem(mine * each, rows * lons // LANES), each, 0)
+    place = lax.rem(mine + blocks - lead, blocks)
+    own_decay = lax.dynamic_slice_in_dim(tiles, lax.rem(place * each, rows * lons // LANES), each, 0)
 
     term, relaxed, ahead = pl.pallas_call(
         inner_kernel,
@@ -242,7 +258,7 @@
         scratch_shapes=[pltpu.VMEM(flat.shape, jnp.float32), pltpu.SemaphoreType.DMA((4,))],
         input_output_aliases={5: 0},
         compiler_params=params,
-    )(turn, state, first, second, coarse_decay, term, relaxed, ahead)
+    )(turn, state, second, first, coarse_decay, term, relaxed, ahead)
 
     def shifted(x, by):
         return lax.ppermute(x, "tm", [(i, (i + by) % blocks) for i in range(blocks)])
@@ -256,23 +272,21 @@
         compiler_params=params,
         cost_estimate=long(10**6),
     )(relaxed, ahead)
-    term = lax.all_to_all(term.reshape(blocks, -1), "tm", 0, 0, tiled=True)
     value = pl.pallas_call(
-        functools.partial(solve_kernel, blocks),
+        functools.partial(solve_kernel, blocks, lead),
         out_shape=flat,
         in_specs=[vmem, vmem],
         out_specs=hbm,
         scratch_shapes=[pltpu.VMEM(flat.shape, jnp.float32), pltpu.SemaphoreType.DMA((4,))],
         compiler_params=params,
-    )(own_decay, term.reshape(-1, LANES))
-    value = lax.all_to_all(value.reshape(blocks, -1), "tm", 0, 0, tiled=True)
+    )(own_decay, exchanged(term))
     corrected = pl.pallas_call(
         finish_kernel,
         out_shape=f32((1, planes, rows, lons)),
         in_specs=[vmem] * 3,
         out_specs=vmem,
         compiler_params=params,
-    )(turn, value.reshape(-1, LANES), relaxed)
+    )(turn, exchanged(value), relaxed)
     return (corrected, residual)
 
 

time: 64.8 us -> 61.6 us (0.951)
  waiting for transfers between devices: 18.9 us -> 6.26 us
  starting transfers between devices: 37.5 us -> 47.1 us
    all_to_all x2, waiting for transfers between devices: 17.1 us -> 2.42 us  [exchanged(): lax.all_to_all(x.reshape(blocks, -1), 'tm', 0, 0, axis_index_groups=place...]
    all_to_all x2, starting transfers between devices: 22.6 us -> 34.2 us  [exchanged(): lax.all_to_all(x.reshape(blocks, -1), 'tm', 0, 0, axis_index_groups=place...]
    ppermute x1, starting transfers between devices: 4.03 us -> 1.92 us  [on_device(): first = lax.ppermute(jnp.where(even, high, low), 'lat', inner)]
    ppermute x2, starting transfers between devices: 6.63 us -> 4.66 us  [shifted(): lax.ppermute(x, 'tm', [(i, (i + by) % blocks) for i in range(blocks)])]
    ppermute x1, starting transfers between devices: 4.27 us -> 6.23 us  [on_device(): second = lax.ppermute(jnp.where(even, low, high), 'lat', outer)]
    ppermute x2, waiting for transfers between devices: 1.63 us -> 3.36 us  [shifted(): lax.ppermute(x, 'tm', [(i, (i + by) % blocks) for i in range(blocks)])]
where the time goes in v2:
time: 61.6 us; the launch traced here: 61.3 us
  starting transfers between devices  47.1 us (76%)
  waiting for transfers between devices  6.26 us (10%)
  Pallas kernels  6.09 us (10%)
  other arithmetic  1.02 us (2%)
  between operations  0.81 us (1%)
    all_to_all x2, starting transfers between devices, exchanged(): lax.all_to_all(x.reshape(blocks, -1), 'tm', 0, 0, axis_index_groups=place...  34.2 us
    ppermute x1, starting transfers between devices, on_device(): second = lax.ppermute(jnp.where(even, low, high), 'lat', outer)  6.23 us
    ppermute x2, starting transfers between devices, shifted(): lax.ppermute(x, 'tm', [(i, (i + by) % blocks) for i in range(blocks)])  4.66 us
    ppermute x2, waiting for transfers between devices, shifted(): lax.ppermute(x, 'tm', [(i, (i + by) % blocks) for i in range(blocks)])  3.36 us
    all_to_all x2, waiting for transfers between devices, exchanged(): lax.all_to_all(x.reshape(blocks, -1), 'tm', 0, 0, axis_index_groups=place...  2.42 us
    pallas_call x1, Pallas kernels, on_device(): pl.pallas_call(inner_kernel, out_shape=(flat, whole, whole), in_specs=[vm...  2.13 us
    ppermute x1, starting transfers between devices, on_device(): first = lax.ppermute(jnp.where(even, high, low), 'lat', inner)  1.92 us
    pallas_call x1, Pallas kernels, on_device(): pl.pallas_call(edge_kernel, out_shape=(flat, whole, whole), in_specs=[vme...  1.76 us
  transfers between devices with their start and end apart: 6, of which 4 were waited for; matrix products, arithmetic and copies ran while one was open for 0% of the time, Pallas kernels for 6%

profile of v2, /device:TPU:1, one launch (start us, length us, event | category | flops | bytes accessed | tf_op | source)
XLA Modules:
  0.0 61.3 jit_solution(7568408820831140754)
XLA Ops:
  0.6 0.0 copy-start.1
  0.7 1.0 %bitcast_select_fusion.state_ref = f32[3,64,256]{2,1,0:T(8,128)S(1)} fusion(f32[3,64,256]{2,1,0:T(8,128)} %param.5, f32[1,3,64,256]{3,2,1,0:T(8,128)} %param.4, pred[]{:T(512)S(6)} %eq.8), kind=kLoop, calls=%fused_computation | loop fusion | flops 49152 | bytes 589825 | tf_op jit(solution)/shard_map/jit(_where)/select_n | solution.py:230
  1.7 0.0 copy-start
  1.7 6.2 %collective-permute-start = (f32[3,8,256]{2,1,0:T(8,128)S(1)}, f32[3,8,256]{2,1,0:T(8,128)S(1)}, u32[]{:S(2)}, u32[]{:S(2)}) collective-permute-start(f32[3,8,256]{2,1,0:T(8,128)S(1)} %get-tuple-element.15), channel_id=1, source_target_pairs={{0,7},{1,2},{2,1},{3,4},{4,3},{5,6},{6,5},{7,0},{8,15},{9,10},{10,... | collective-permute-start | bytes 73736 | tf_op jit(solution)/shard_map/ppermute | solution.py:235
  7.9 1.9 %collective-permute-start.1 = (f32[3,8,256]{2,1,0:T(8,128)S(1)}, f32[3,8,256]{2,1,0:T(8,128)S(1)}, u32[]{:S(2)}, u32[]{:S(2)}) collective-permute-start(f32[3,8,256]{2,1,0:T(8,128)S(1)} %get-tuple-element.14), channel_id=1, source_target_pairs={{0,1},{1,0},{2,3},{3,2},{4,5},{5,4},{6,7},{7,6},{8,9},{9,8},{10,11... | collective-permute-start | bytes 73736 | tf_op jit(solution)/shard_map/ppermute | solution.py:236
  9.8 0.0 copy-done.1
  9.9 0.0 copy-done
  9.9 2.1 %shard_map.59 = (f32[384,128]{1,0:T(8,128)}, f32[3,64,256]{2,1,0:T(8,128)S(1)}, f32[3,64,256]{2,1,0:T(8,128)S(1)}) custom-call(f32[128,128]{1,0:T(8,128)S(1)} %copy-done.1, f32[3,64,256]{2,1,0:T(8,128)S(1)} %bitcast_select_fusion.state_ref, f32[64,256]{1,0:T(8,128)S(1)} %copy-done), custom_call_target="tpu_custom_call" | custom-call | flops 49152000 | bytes 393216 | tf_op jit(solution)/shard_map/pallas_call | solution.py:244
  12.0 0.0 collective-permute-done.second_ref
  12.0 0.5 collective-permute-done.1.first_ref
  12.5 1.8 %shard_map.60 = (f32[384,128]{1,0:T(8,128)}, f32[3,64,256]{2,1,0:T(8,128)S(1)}, f32[3,64,256]{2,1,0:T(8,128)S(1)}) custom-call(f32[128,128]{1,0:T(8,128)S(1)} %copy-done.1, f32[3,64,256]{2,1,0:T(8,128)S(1)} %bitcast_select_fusion.state_ref, f32[3,8,256]{2,1,0:T(8,128)S(1)} %collective-permute-done.second_ref, ...), custom_call_target="tpu_custom_call", output_to_operand_aliasing={{0}: (5, {})} | custom-call | tf_op jit(solution)/shard_map/pallas_call | solution.py:253
  14.3 21.0 %all-to-all-start = ((f32[64,1,768]{2,1,0:T(1,128)}), f32[64,1,768]{2,1,0:T(1,128)S(1)}, u32[]{:S(2)}, u32[]{:S(2)}) async-start(f32[64,1,768]{2,1,0:T(1,128)} %bitcast.6), calls=%async_computation | async-start | bytes 393216 | tf_op jit(solution)/shard_map/all_to_all | solution.py:223
  35.2 2.5 %collective-permute-start.2 = (f32[3,64,256]{2,1,0:T(8,128)S(1)}, f32[3,64,256]{2,1,0:T(8,128)S(1)}, u32[]{:S(2)}, u32[]{:S(2)}) collective-permute-start(f32[3,64,256]{2,1,0:T(8,128)S(1)} %get-tuple-element.12), channel_id=1, source_target_pairs={{0,8},{8,16},{16,24},{24,32},{32,40},{40,48},{48,56},{56,64},{64,7... | collective-permute-start | bytes 589832 | tf_op jit(solution)/shard_map/ppermute | solution.py:264
  37.7 2.2 %collective-permute-start.3 = (f32[3,64,256]{2,1,0:T(8,128)S(1)}, f32[3,64,256]{2,1,0:T(8,128)S(1)}, u32[]{:S(2)}, u32[]{:S(2)}) collective-permute-start(f32[3,64,256]{2,1,0:T(8,128)S(1)} %get-tuple-element.13), channel_id=1, source_target_pairs={{0,16},{8,24},{16,32},{24,40},{32,48},{40,56},{48,64},{56,72},{64,... | collective-permute-start | bytes 589832 | tf_op jit(solution)/shard_map/ppermute | solution.py:264
  40.0 0.6 all-to-all-done
  40.5 0.8 %shard_map.61 = f32[384,128]{1,0:T(8,128)} custom-call(f32[6,128]{1,0:T(8,128)S(1)} %fusion.decay_ref, f32[384,128]{1,0:T(8,128)S(1)} %bitcast.11), custom_call_target="tpu_custom_call" | custom-call | tf_op jit(solution)/shard_map/pallas_call | solution.py:275
  41.3 13.3 %all-to-all-start.1 = ((f32[64,1,768]{2,1,0:T(1,128)}), f32[64,1,768]{2,1,0:T(1,128)S(1)}, u32[]{:S(2)}, u32[]{:S(2)}) async-start(f32[64,1,768]{2,1,0:T(1,128)} %bitcast.8), calls=%async_computation.1 | async-start | bytes 393216 | tf_op jit(solution)/shard_map/all_to_all | solution.py:223
  54.6 0.0 collective-permute-done.2.relaxed_ref
  54.6 3.4 %collective-permute-done.3.ahead_ref = f32[3,64,256]{2,1,0:T(8,128)S(1)} collective-permute-done((f32[3,64,256]{2,1,0:T(8,128)S(1)}, f32[3,64,256]{2,1,0:T(8,128)S(1)}, u32[]{:S(2)}, u32[]{:S(2)}) %collective-permute-start.3) | collective-permute-done | bytes 196640 | tf_op jit(solution)/shard_map/ppermute | solution.py:264
  58.0 0.7 %shard_map.63 = f32[1,3,64,256]{3,2,1,0:T(8,128)} custom-call(f32[3,64,256]{2,1,0:T(8,128)S(1)} %collective-permute-done.2.relaxed_ref, f32[3,64,256]{2,1,0:T(8,128)S(1)} %collective-permute-done.3.ahead_ref), custom_call_target="tpu_custom_call" | custom-call | flops 49152000000 | bytes 393216 | tf_op jit(solution)/shard_map/pallas_call | solution.py:267
  58.7 1.8 %all-to-all-done.1 = f32[64,1,768]{2,1,0:T(1,128)S(1)} async-done(((f32[64,1,768]{2,1,0:T(1,128)}), f32[64,1,768]{2,1,0:T(1,128)S(1)}, u32[]{:S(2)}, u32[]{:S(2)}) %all-to-all-start.1) | async-done | bytes 196640 | tf_op jit(solution)/shard_map/all_to_all | solution.py:223
  60.5 0.7 %shard_map.62 = f32[1,3,64,256]{3,2,1,0:T(8,128)} custom-call(f32[128,128]{1,0:T(8,128)S(1)} %copy-done.1, f32[384,128]{1,0:T(8,128)S(1)} %bitcast.12, f32[3,64,256]{2,1,0:T(8,128)S(1)} %collective-permute-done.2.relaxed_ref), custom_call_target="tpu_custom_call" | custom-call | tf_op jit(solution)/shard_map/pallas_call | solution.py:283
  (3 shorter events, 0.0 us)
Async XLA Ops:
  0.6 9.2 %copy-start.1 = (f32[128,128]{1,0:T(8,128)S(1)}, f32[128,128]{1,0:T(8,128)}, u32[]{:S(2)}) copy-start(f32[128,128]{1,0:T(8,128)} %constant.42.clone.turn_ref) | copy-start | bytes 196612
  1.7 8.2 %copy-start = (f32[64,256]{1,0:T(8,128)S(1)}, f32[64,256]{1,0:T(8,128)}, u32[]{:S(2)}) copy-start(f32[64,256]{1,0:T(8,128)} %decay_ref.3) | copy-start | bytes 196612
  1.7 10.3 %collective-permute-start = (f32[3,8,256]{2,1,0:T(8,128)S(1)}, f32[3,8,256]{2,1,0:T(8,128)S(1)}, u32[]{:S(2)}, u32[]{:S(2)}) collective-permute-start(f32[3,8,256]{2,1,0:T(8,128)S(1)} %get-tuple-element.15), channel_id=1, source_target_pairs={{0,7},{1,2},{2,1},{3,4},{4,3},{5,6},{6,5},{7,0},{8,15},{9,10},{10,... | collective-permute-start | bytes 73736 | tf_op jit(solution)/shard_map/ppermute | solution.py:235
  7.9 4.6 %collective-permute-start.1 = (f32[3,8,256]{2,1,0:T(8,128)S(1)}, f32[3,8,256]{2,1,0:T(8,128)S(1)}, u32[]{:S(2)}, u32[]{:S(2)}) collective-permute-start(f32[3,8,256]{2,1,0:T(8,128)S(1)} %get-tuple-element.14), channel_id=1, source_target_pairs={{0,1},{1,0},{2,3},{3,2},{4,5},{5,4},{6,7},{7,6},{8,9},{9,8},{10,11... | collective-permute-start | bytes 73736 | tf_op jit(solution)/shard_map/ppermute | solution.py:236
  14.3 26.3 %all-to-all-start = ((f32[64,1,768]{2,1,0:T(1,128)}), f32[64,1,768]{2,1,0:T(1,128)S(1)}, u32[]{:S(2)}, u32[]{:S(2)}) async-start(f32[64,1,768]{2,1,0:T(1,128)} %bitcast.6), calls=%async_computation | async-start | bytes 393216 | tf_op jit(solution)/shard_map/all_to_all | solution.py:223
  35.2 19.4 %collective-permute-start.2 = (f32[3,64,256]{2,1,0:T(8,128)S(1)}, f32[3,64,256]{2,1,0:T(8,128)S(1)}, u32[]{:S(2)}, u32[]{:S(2)}) collective-permute-start(f32[3,64,256]{2,1,0:T(8,128)S(1)} %get-tuple-element.12), channel_id=1, source_target_pairs={{0,8},{8,16},{16,24},{24,32},{32,40},{40,48},{48,56},{56,64},{64,7... | collective-permute-start | bytes 589832 | tf_op jit(solution)/shard_map/ppermute | solution.py:264
  37.7 20.3 %collective-permute-start.3 = (f32[3,64,256]{2,1,0:T(8,128)S(1)}, f32[3,64,256]{2,1,0:T(8,128)S(1)}, u32[]{:S(2)}, u32[]{:S(2)}) collective-permute-start(f32[3,64,256]{2,1,0:T(8,128)S(1)} %get-tuple-element.13), channel_id=1, source_target_pairs={{0,16},{8,24},{16,32},{24,40},{32,48},{40,56},{48,64},{56,72},{64,... | collective-permute-start | bytes 589832 | tf_op jit(solution)/shard_map/ppermute | solution.py:264
  41.3 19.2 %all-to-all-start.1 = ((f32[64,1,768]{2,1,0:T(1,128)}), f32[64,1,768]{2,1,0:T(1,128)S(1)}, u32[]{:S(2)}, u32[]{:S(2)}) async-start(f32[64,1,768]{2,1,0:T(1,128)} %bitcast.8), calls=%async_computation.1 | async-start | bytes 393216 | tf_op jit(solution)/shard_map/all_to_all | solution.py:223

commit v3 on v2

--- a/solution.py
+++ b/solution.py
@@ -151,14 +151,15 @@
         copy.wait()
 
 
-def solve_kernel(blocks, lead, decay_ref, term_ref, value_ref, values, sem):
+def solve_kernel(places, decay_ref, term_ref, value_ref, values, sem):
     shrink = jnp.exp(-decay_ref[...])
     each = shrink.shape[0]
     parts = sem.shape[0]
 
+    blocks = len(places)
+
     def at(slot):
-        place = (slot - lead) % blocks
-        return slice(place * each, (place + 1) * each)
+        return slice(places[slot] * each, (places[slot] + 1) * each)
 
     value = term_ref[at(blocks - 1)]
     size = each * blocks // parts
@@ -167,8 +168,8 @@
         if slot >= 2:
             value = shrink * value + term_ref[at(slot - 2)]
         values[at(slot)] = value
-        done.add((slot - lead) % blocks * parts // blocks)
-        later = {(more - lead) % blocks * parts // blocks for more in range(slot + 1, blocks)}
+        done.add(places[slot] * parts // blocks)
+        later = {place * parts // blocks for place in places[slot + 1 :]}
         for k in sorted(done - later):
             done.remove(k)
             part = pl.ds(k * size, size)
@@ -216,12 +217,13 @@
     whole, flat = f32((planes, rows, lons)), f32((size // LANES, LANES))
     params = pltpu.CompilerParams(vmem_limit_bytes=32 << 20)
     turn = jnp.asarray(turns(blocks))
-    lead = 5 * blocks // 8
-    places = [[(place + lead) % blocks for place in range(blocks)]]
+    lead = 11 * blocks // 16
+    order = [lead] + [block for block in range(blocks) if block != lead]
+    places = [order.index(block) for block in range(blocks)]
 
     def exchanged(x):
         return lax.all_to_all(
-            x.reshape(blocks, -1), "tm", 0, 0, axis_index_groups=places, tiled=True
+            x.reshape(blocks, -1), "tm", 0, 0, axis_index_groups=[order], tiled=True
         ).reshape(-1, LANES)
 
     def long(steps):
@@ -238,7 +240,7 @@
     tiles = coarse_decay.reshape(rows // 8, 8, lons // LANES, LANES).transpose(0, 2, 1, 3)
     tiles = tiles.reshape(-1, LANES)
     tiles = jnp.concatenate([tiles, tiles[:each]], axis=0)
-    place = lax.rem(mine + blocks - lead, blocks)
+    place = jnp.where(mine == lead, 0, jnp.where(mine < lead, mine + 1, mine))
     own_decay = lax.dynamic_slice_in_dim(tiles, lax.rem(place * each, rows * lons // LANES), each, 0)
 
     term, relaxed, ahead = pl.pallas_call(
@@ -260,10 +262,8 @@
         compiler_params=params,
     )(turn, state, second, first, coarse_decay, term, relaxed, ahead)
 
-    def shifted(x, by):
-        return lax.ppermute(x, "tm", [(i, (i + by) % blocks) for i in range(blocks)])
-
-    relaxed, ahead = shifted(relaxed, 1), shifted(ahead, 2)
+    relaxed = lax.ppermute(relaxed, "tm", [(i, (i + 1) % blocks) for i in range(blocks)])
+    ahead = lax.ppermute(ahead, "tm", [(i, (i + 2) % blocks) for i in range(blocks) if i != blocks - 2])
     residual = pl.pallas_call(
         residual_kernel,
         out_shape=f32((1, planes, rows, lons)),
@@ -273,7 +273,7 @@
         cost_estimate=long(10**6),
     )(relaxed, ahead)
     value = pl.pallas_call(
-        functools.partial(solve_kernel, blocks, lead),
+        functools.partial(solve_kernel, places),
         out_shape=flat,
         in_specs=[vmem, vmem],
         out_specs=hbm,

time: 61.6 us -> 61.1 us (level)
  starting transfers between devices: 47.1 us -> 45.3 us
  waiting for transfers between devices: 6.26 us -> 7.48 us
    all_to_all x2, waiting for transfers between devices: 2.42 us -> 7 us  [exchanged(): lax.all_to_all(x.reshape(blocks, -1), 'tm', 0, 0, axis_index_groups=[orde...]
    all_to_all x2, starting transfers between devices: 34.2 us -> 30.7 us  [exchanged(): lax.all_to_all(x.reshape(blocks, -1), 'tm', 0, 0, axis_index_groups=[orde...]
    ppermute x2, waiting for transfers between devices: 3.36 us -> 0.01 us  [the longest x1 0.01 us: on_device(): lax.ppermute(relaxed, 'tm', [(i, (i + 1) % blocks) for i in range(blocks)])]
    ppermute x2, starting transfers between devices: 4.66 us -> 6.46 us  [the longest x1 3.35 us: on_device(): lax.ppermute(relaxed, 'tm', [(i, (i + 1) % blocks) for i in range(blocks)])]
  transfers between devices with their start and end apart: 6 -> 6, of which waited for: 4 -> 3; matrix products, arithmetic and copies ran while one was open for 0% -> 0% of each run, Pallas kernels for 6% -> 6%
where the time goes in v3:
time: 61.1 us; the launch traced here: 60.7 us
  starting transfers between devices  45.3 us (74%)
  waiting for transfers between devices  7.48 us (12%)
  Pallas kernels  6.1 us (10%)
  other arithmetic  1.02 us (2%)
  between operations  0.82 us (1%)
    all_to_all x2, starting transfers between devices, exchanged(): lax.all_to_all(x.reshape(blocks, -1), 'tm', 0, 0, axis_index_groups=[orde...  30.7 us
    all_to_all x2, waiting for transfers between devices, exchanged(): lax.all_to_all(x.reshape(blocks, -1), 'tm', 0, 0, axis_index_groups=[orde...  7 us
    ppermute x1, starting transfers between devices, on_device(): second = lax.ppermute(jnp.where(even, low, high), 'lat', outer)  6.23 us
    ppermute x1, starting transfers between devices, on_device(): lax.ppermute(relaxed, 'tm', [(i, (i + 1) % blocks) for i in range(blocks)])  3.35 us
    ppermute x1, starting transfers between devices, on_device(): lax.ppermute(ahead, 'tm', [(i, (i + 2) % blocks) for i in range(blocks) i...  3.1 us
    pallas_call x1, Pallas kernels, on_device(): pl.pallas_call(inner_kernel, out_shape=(flat, whole, whole), in_specs=[vm...  2.13 us
    ppermute x1, starting transfers between devices, on_device(): first = lax.ppermute(jnp.where(even, high, low), 'lat', inner)  1.92 us
    pallas_call x1, Pallas kernels, on_device(): pl.pallas_call(edge_kernel, out_shape=(flat, whole, whole), in_specs=[vme...  1.76 us
  transfers between devices with their start and end apart: 6, of which 3 were waited for; matrix products, arithmetic and copies ran while one was open for 0% of the time, Pallas kernels for 6%

profile of v3, /device:TPU:1, one launch (start us, length us, event | category | flops | bytes accessed | tf_op | source)
XLA Modules:
  0.0 60.7 jit_solution(10900404152233623503)
XLA Ops:
  0.6 0.0 copy-start.1
  0.7 1.0 %bitcast_select_fusion.state_ref = f32[3,64,256]{2,1,0:T(8,128)S(1)} fusion(f32[3,64,256]{2,1,0:T(8,128)} %param.5, f32[1,3,64,256]{3,2,1,0:T(8,128)} %param.4, pred[]{:T(512)S(6)} %eq.12), kind=kLoop, calls=%fused_computation | loop fusion | flops 49152 | bytes 589825 | tf_op jit(solution)/shard_map/jit(_where)/select_n | solution.py:232
  1.7 0.0 copy-start
  1.7 6.2 %collective-permute-start = (f32[3,8,256]{2,1,0:T(8,128)S(1)}, f32[3,8,256]{2,1,0:T(8,128)S(1)}, u32[]{:S(2)}, u32[]{:S(2)}) collective-permute-start(f32[3,8,256]{2,1,0:T(8,128)S(1)} %get-tuple-element.15), channel_id=1, source_target_pairs={{0,7},{1,2},{2,1},{3,4},{4,3},{5,6},{6,5},{7,0},{8,15},{9,10},{10,... | collective-permute-start | bytes 73736 | tf_op jit(solution)/shard_map/ppermute | solution.py:237
  7.9 1.9 %collective-permute-start.1 = (f32[3,8,256]{2,1,0:T(8,128)S(1)}, f32[3,8,256]{2,1,0:T(8,128)S(1)}, u32[]{:S(2)}, u32[]{:S(2)}) collective-permute-start(f32[3,8,256]{2,1,0:T(8,128)S(1)} %get-tuple-element.14), channel_id=1, source_target_pairs={{0,1},{1,0},{2,3},{3,2},{4,5},{5,4},{6,7},{7,6},{8,9},{9,8},{10,11... | collective-permute-start | bytes 73736 | tf_op jit(solution)/shard_map/ppermute | solution.py:238
  9.8 0.0 copy-done.1
  9.9 0.0 copy-done
  9.9 2.1 %shard_map.59 = (f32[384,128]{1,0:T(8,128)}, f32[3,64,256]{2,1,0:T(8,128)S(1)}, f32[3,64,256]{2,1,0:T(8,128)S(1)}) custom-call(f32[128,128]{1,0:T(8,128)S(1)} %copy-done.1, f32[3,64,256]{2,1,0:T(8,128)S(1)} %bitcast_select_fusion.state_ref, f32[64,256]{1,0:T(8,128)S(1)} %copy-done), custom_call_target="tpu_custom_call" | custom-call | flops 49152000 | bytes 393216 | tf_op jit(solution)/shard_map/pallas_call | solution.py:246
  12.0 0.0 collective-permute-done.second_ref
  12.0 0.5 collective-permute-done.1.first_ref
  12.5 1.8 %shard_map.60 = (f32[384,128]{1,0:T(8,128)}, f32[3,64,256]{2,1,0:T(8,128)S(1)}, f32[3,64,256]{2,1,0:T(8,128)S(1)}) custom-call(f32[128,128]{1,0:T(8,128)S(1)} %copy-done.1, f32[3,64,256]{2,1,0:T(8,128)S(1)} %bitcast_select_fusion.state_ref, f32[3,8,256]{2,1,0:T(8,128)S(1)} %collective-permute-done.second_ref, ...), custom_call_target="tpu_custom_call", output_to_operand_aliasing={{0}: (5, {})} | custom-call | tf_op jit(solution)/shard_map/pallas_call | solution.py:255
  14.3 19.2 %all-to-all-start = ((f32[64,1,768]{2,1,0:T(1,128)}), f32[64,1,768]{2,1,0:T(1,128)S(1)}, u32[]{:S(2)}, u32[]{:S(2)}) async-start(f32[64,1,768]{2,1,0:T(1,128)} %bitcast.6), calls=%async_computation | async-start | bytes 393216 | tf_op jit(solution)/shard_map/all_to_all | solution.py:225
  33.5 3.4 %collective-permute-start.2 = (f32[3,64,256]{2,1,0:T(8,128)S(1)}, f32[3,64,256]{2,1,0:T(8,128)S(1)}, u32[]{:S(2)}, u32[]{:S(2)}) collective-permute-start(f32[3,64,256]{2,1,0:T(8,128)S(1)} %get-tuple-element.12), channel_id=1, source_target_pairs={{0,8},{8,16},{16,24},{24,32},{32,40},{40,48},{48,56},{56,64},{64,7... | collective-permute-start | bytes 589832 | tf_op jit(solution)/shard_map/ppermute | solution.py:265
  36.8 3.1 %collective-permute-start.3 = (f32[3,64,256]{2,1,0:T(8,128)S(1)}, f32[3,64,256]{2,1,0:T(8,128)S(1)}, u32[]{:S(2)}, u32[]{:S(2)}) collective-permute-start(f32[3,64,256]{2,1,0:T(8,128)S(1)} %get-tuple-element.13), channel_id=1, source_target_pairs={{0,16},{8,24},{16,32},{24,40},{32,48},{40,56},{48,64},{56,72},{64,... | collective-permute-start | bytes 589832 | tf_op jit(solution)/shard_map/ppermute | solution.py:266
  40.0 0.5 all-to-all-done
  40.5 0.8 %shard_map.61 = f32[384,128]{1,0:T(8,128)} custom-call(f32[6,128]{1,0:T(8,128)S(1)} %fusion.decay_ref, f32[384,128]{1,0:T(8,128)S(1)} %bitcast.11), custom_call_target="tpu_custom_call" | custom-call | tf_op jit(solution)/shard_map/pallas_call | solution.py:275
  41.3 11.5 %all-to-all-start.1 = ((f32[64,1,768]{2,1,0:T(1,128)}), f32[64,1,768]{2,1,0:T(1,128)S(1)}, u32[]{:S(2)}, u32[]{:S(2)}) async-start(f32[64,1,768]{2,1,0:T(1,128)} %bitcast.8), calls=%async_computation.1 | async-start | bytes 393216 | tf_op jit(solution)/shard_map/all_to_all | solution.py:225
  52.8 0.0 collective-permute-done.2.relaxed_ref
  52.8 0.0 collective-permute-done.3.ahead_ref
  52.8 0.7 %shard_map.63 = f32[1,3,64,256]{3,2,1,0:T(8,128)} custom-call(f32[3,64,256]{2,1,0:T(8,128)S(1)} %collective-permute-done.2.relaxed_ref, f32[3,64,256]{2,1,0:T(8,128)S(1)} %collective-permute-done.3.ahead_ref), custom_call_target="tpu_custom_call" | custom-call | flops 49152000000 | bytes 393216 | tf_op jit(solution)/shard_map/pallas_call | solution.py:267
  53.5 6.5 %all-to-all-done.1 = f32[64,1,768]{2,1,0:T(1,128)S(1)} async-done(((f32[64,1,768]{2,1,0:T(1,128)}), f32[64,1,768]{2,1,0:T(1,128)S(1)}, u32[]{:S(2)}, u32[]{:S(2)}) %all-to-all-start.1) | async-done | bytes 196640 | tf_op jit(solution)/shard_map/all_to_all | solution.py:225
  60.0 0.7 %shard_map.62 = f32[1,3,64,256]{3,2,1,0:T(8,128)} custom-call(f32[128,128]{1,0:T(8,128)S(1)} %copy-done.1, f32[384,128]{1,0:T(8,128)S(1)} %bitcast.12, f32[3,64,256]{2,1,0:T(8,128)S(1)} %collective-permute-done.2.relaxed_ref), custom_call_target="tpu_custom_call" | custom-call | tf_op jit(solution)/shard_map/pallas_call | solution.py:283
  (3 shorter events, 0.0 us)
Async XLA Ops:
  0.6 9.2 %copy-start.1 = (f32[128,128]{1,0:T(8,128)S(1)}, f32[128,128]{1,0:T(8,128)}, u32[]{:S(2)}) copy-start(f32[128,128]{1,0:T(8,128)} %constant.38.clone.turn_ref) | copy-start | bytes 196612
  1.7 8.2 %copy-start = (f32[64,256]{1,0:T(8,128)S(1)}, f32[64,256]{1,0:T(8,128)}, u32[]{:S(2)}) copy-start(f32[64,256]{1,0:T(8,128)} %decay_ref.3) | copy-start | bytes 196612
  1.7 10.3 %collective-permute-start = (f32[3,8,256]{2,1,0:T(8,128)S(1)}, f32[3,8,256]{2,1,0:T(8,128)S(1)}, u32[]{:S(2)}, u32[]{:S(2)}) collective-permute-start(f32[3,8,256]{2,1,0:T(8,128)S(1)} %get-tuple-element.15), channel_id=1, source_target_pairs={{0,7},{1,2},{2,1},{3,4},{4,3},{5,6},{6,5},{7,0},{8,15},{9,10},{10,... | collective-permute-start | bytes 73736 | tf_op jit(solution)/shard_map/ppermute | solution.py:237
  7.9 4.6 %collective-permute-start.1 = (f32[3,8,256]{2,1,0:T(8,128)S(1)}, f32[3,8,256]{2,1,0:T(8,128)S(1)}, u32[]{:S(2)}, u32[]{:S(2)}) collective-permute-start(f32[3,8,256]{2,1,0:T(8,128)S(1)} %get-tuple-element.14), channel_id=1, source_target_pairs={{0,1},{1,0},{2,3},{3,2},{4,5},{5,4},{6,7},{7,6},{8,9},{9,8},{10,11... | collective-permute-start | bytes 73736 | tf_op jit(solution)/shard_map/ppermute | solution.py:238
  14.3 26.2 %all-to-all-start = ((f32[64,1,768]{2,1,0:T(1,128)}), f32[64,1,768]{2,1,0:T(1,128)S(1)}, u32[]{:S(2)}, u32[]{:S(2)}) async-start(f32[64,1,768]{2,1,0:T(1,128)} %bitcast.6), calls=%async_computation | async-start | bytes 393216 | tf_op jit(solution)/shard_map/all_to_all | solution.py:225
  33.5 19.3 %collective-permute-start.2 = (f32[3,64,256]{2,1,0:T(8,128)S(1)}, f32[3,64,256]{2,1,0:T(8,128)S(1)}, u32[]{:S(2)}, u32[]{:S(2)}) collective-permute-start(f32[3,64,256]{2,1,0:T(8,128)S(1)} %get-tuple-element.12), channel_id=1, source_target_pairs={{0,8},{8,16},{16,24},{24,32},{32,40},{40,48},{48,56},{56,64},{64,7... | collective-permute-start | bytes 589832 | tf_op jit(solution)/shard_map/ppermute | solution.py:265
  36.8 16.0 %collective-permute-start.3 = (f32[3,64,256]{2,1,0:T(8,128)S(1)}, f32[3,64,256]{2,1,0:T(8,128)S(1)}, u32[]{:S(2)}, u32[]{:S(2)}) collective-permute-start(f32[3,64,256]{2,1,0:T(8,128)S(1)} %get-tuple-element.13), channel_id=1, source_target_pairs={{0,16},{8,24},{16,32},{24,40},{32,48},{40,56},{48,64},{56,72},{64,... | collective-permute-start | bytes 589832 | tf_op jit(solution)/shard_map/ppermute | solution.py:266
  41.3 18.7 %all-to-all-start.1 = ((f32[64,1,768]{2,1,0:T(1,128)}), f32[64,1,768]{2,1,0:T(1,128)S(1)}, u32[]{:S(2)}, u32[]{:S(2)}) async-start(f32[64,1,768]{2,1,0:T(1,128)} %bitcast.8), calls=%async_computation.1 | async-start | bytes 393216 | tf_op jit(solution)/shard_map/all_to_all | solution.py:225

commit v4 on v3

--- a/solution.py
+++ b/solution.py
@@ -93,62 +93,34 @@
                 term_ref[to : to + 8] = term
 
 
-def inner_kernel(turn_ref, state_ref, decay_ref, term_ref, relaxed_ref, ahead_ref, term, sem):
-    rows = state_ref.shape[1]
-    relaxed, ahead = two_blocks([state_ref[plane] for plane in range(3)])
-    for plane in range(3):
-        relaxed_ref[plane] = relaxed[plane]
-        ahead_ref[plane] = ahead[plane]
-    put_forcing(turn_ref, decay_ref, relaxed_ref, ahead_ref, term, range(8, rows - 8, 8))
-    edge = 8 * decay_ref.shape[1] // LANES
-    per_plane = term.shape[0] // 3
-    copies = []
-    for plane in range(3):
-        part = pl.ds(plane * per_plane + edge, per_plane - 2 * edge)
-        copies.append(pltpu.make_async_copy(term.at[part], term_ref.at[part], sem.at[plane]))
-        copies[-1].start()
-    for copy in copies:
-        copy.wait()
-
-
-def edge_kernel(
-    turn_ref, state_ref, second_ref, first_ref, decay_ref, term_in, relaxed_in, ahead_in,
-    term_ref, relaxed_ref, ahead_ref, term, sem,
+def relax_kernel(
+    turn_ref, state_ref, second_ref, pair_ref, decay_ref, term_ref, relaxed_ref, ahead_ref, term, sem
 ):
     even = lax.rem(lax.axis_index("lat"), 2) == 0
-    rows = state_ref.shape[1]
+    rows, lons = state_ref.shape[1:]
     state = []
     for plane in range(3):
-        first, second = first_ref[plane], second_ref[plane]
+        first = jnp.where(even, pair_ref[1, plane], pair_ref[0, plane])
+        second = second_ref[plane]
         below = jnp.where(even, second, first)
         above = jnp.where(even, first, second)
-        low, high = state_ref[plane, : 2 * HALO], state_ref[plane, rows - 2 * HALO :]
-        state.append(jnp.concatenate([below, low, high, above], axis=0))
+        state.append(jnp.concatenate([below, state_ref[plane], above], axis=0))
     relaxed, ahead = two_blocks(state)
-    lons = decay_ref.shape[1]
-    edge = 8 * lons // LANES
     per_plane = term.shape[0] // 3
-    for row, at in ((0, HALO), (rows - 8, 4 * HALO)):
+    for row in range(0, rows, 8):
         for col in range(0, lons, LANES):
             cols = slice(col, col + LANES)
+            at = row + HALO
             tiles = [[a[at : at + 8, cols] for a in state] for state in (relaxed, ahead)]
             to = row * lons // LANES + col * 8 // LANES
             for plane, value in enumerate(forcing(turn_ref, decay_ref[row : row + 8, cols], *tiles)):
                 term[plane * per_plane + to : plane * per_plane + to + 8] = value
-    ends = [0, *(plane * per_plane for plane in (1, 2)), 3 * per_plane]
-    copies = []
-    for k, end in enumerate(ends):
-        start, stop = max(end - edge, 0), min(end + edge, 3 * per_plane)
-        part = pl.ds(start, stop - start)
-        copies.append(pltpu.make_async_copy(term.at[part], term_ref.at[part], sem.at[k]))
-        copies[-1].start()
-    for to, inner, values in ((relaxed_ref, relaxed_in, relaxed), (ahead_ref, ahead_in, ahead)):
+    copy = pltpu.make_async_copy(term, term_ref, sem.at[0])
+    copy.start()
+    for to, values in ((relaxed_ref, relaxed), (ahead_ref, ahead)):
         for plane, value in enumerate(values):
-            to[plane, HALO : rows - HALO] = inner[plane, HALO : rows - HALO]
-            to[plane, :HALO] = value[HALO : 2 * HALO]
-            to[plane, rows - HALO :] = value[4 * HALO : 5 * HALO]
-    for copy in copies:
-        copy.wait()
+            to[plane] = value[HALO : HALO + rows]
+    copy.wait()
 
 
 def solve_kernel(places, decay_ref, term_ref, value_ref, values, sem):
@@ -179,14 +151,25 @@
         copy.wait()
 
 
-def residual_kernel(relaxed_ref, ahead_ref, residual_ref):
-    first = lax.axis_index("tm") == 0
+def pass_kernel(blocks, both_ref, ahead_ref, passed_ref):
+    mine = lax.axis_index("tm")
+    odd = lax.rem(mine, 2) == 1
+    last = mine == blocks - 2
     for plane in range(3):
-        relaxed = relaxed_ref[plane]
-        residual_ref[0, plane] = jnp.where(first, relaxed, ahead_ref[plane]) - relaxed
-
-
-def finish_kernel(turn_ref, value_ref, relaxed_ref, corrected_ref):
+        ahead, other = ahead_ref[plane], both_ref[1, plane]
+        passed_ref[plane] = jnp.where(odd, ahead, jnp.where(last, other, ahead - other))
+
+
+def residual_kernel(both_ref, got_ref, residual_ref):
+    mine = lax.axis_index("tm")
+    odd, first = lax.rem(mine, 2) == 1, mine == 0
+    for plane in range(3):
+        got = got_ref[plane]
+        relaxed = jnp.where(odd, both_ref[0, plane], jnp.where(first, got, 0.0))
+        residual_ref[0, plane] = got - relaxed
+
+
+def finish_kernel(turn_ref, value_ref, got_ref, corrected_ref):
     mine = lax.axis_index("tm")
     first = mine == 0
     cos, sin = turn_of(turn_ref, mine)
@@ -201,7 +184,7 @@
             values = (height, cos * zonal + sin * merid, cos * merid - sin * zonal)
             for plane in range(3):
                 block = (plane, slice(row, row + 8), slice(col, col + LANES))
-                corrected_ref[(0, *block)] = jnp.where(first, relaxed_ref[block], values[plane])
+                corrected_ref[(0, *block)] = jnp.where(first, got_ref[block], values[plane])
             at += 8
 
 
@@ -232,10 +215,10 @@
     state = jnp.where(mine == blocks - 1, initial_state, states[0])
     even = slab % 2 == 0
     low, high = state[:, :HALO], state[:, -HALO:]
-    inner = [(i, i ^ 1) for i in range(slabs)]
     outer = [(i, (i - 1 if i % 2 == 0 else i + 1) % slabs) for i in range(slabs)]
     second = lax.ppermute(jnp.where(even, low, high), "lat", outer)
-    first = lax.ppermute(jnp.where(even, high, low), "lat", inner)
+    pairs = [[i, i + 1] for i in range(0, slabs, 2)]
+    pair = lax.all_gather(jnp.where(even, high, low), "lat", axis_index_groups=pairs)
 
     tiles = coarse_decay.reshape(rows // 8, 8, lons // LANES, LANES).transpose(0, 2, 1, 3)
     tiles = tiles.reshape(-1, LANES)
@@ -244,26 +227,23 @@
     own_decay = lax.dynamic_slice_in_dim(tiles, lax.rem(place * each, rows * lons // LANES), each, 0)
 
     term, relaxed, ahead = pl.pallas_call(
-        inner_kernel,
+        relax_kernel,
         out_shape=(flat, whole, whole),
-        in_specs=[vmem] * 3,
+        in_specs=[vmem] * 5,
         out_specs=(hbm, vmem, vmem),
-        scratch_shapes=[pltpu.VMEM(flat.shape, jnp.float32), pltpu.SemaphoreType.DMA((3,))],
-        compiler_params=params,
-        cost_estimate=long(10**3),
-    )(turn, state, coarse_decay)
-    term, relaxed, ahead = pl.pallas_call(
-        edge_kernel,
-        out_shape=(flat, whole, whole),
-        in_specs=[vmem] * 5 + [hbm, vmem, vmem],
-        out_specs=(hbm, vmem, vmem),
-        scratch_shapes=[pltpu.VMEM(flat.shape, jnp.float32), pltpu.SemaphoreType.DMA((4,))],
-        input_output_aliases={5: 0},
-        compiler_params=params,
-    )(turn, state, second, first, coarse_decay, term, relaxed, ahead)
-
-    relaxed = lax.ppermute(relaxed, "tm", [(i, (i + 1) % blocks) for i in range(blocks)])
-    ahead = lax.ppermute(ahead, "tm", [(i, (i + 2) % blocks) for i in range(blocks) if i != blocks - 2])
+        scratch_shapes=[pltpu.VMEM(flat.shape, jnp.float32), pltpu.SemaphoreType.DMA((1,))],
+        compiler_params=params,
+    )(turn, state, second, pair, coarse_decay)
+
+    both = lax.all_gather(relaxed, "tm", axis_index_groups=[[i, i + 1] for i in range(0, blocks, 2)])
+    passed = pl.pallas_call(
+        functools.partial(pass_kernel, blocks),
+        out_shape=whole,
+        in_specs=[vmem, vmem],
+        out_specs=vmem,
+        compiler_params=params,
+    )(both, ahead)
+    got = lax.ppermute(passed, "tm", [(i, (i + 2) % blocks) for i in range(blocks)])
     residual = pl.pallas_call(
         residual_kernel,
         out_shape=f32((1, planes, rows, lons)),
@@ -271,7 +251,7 @@
         out_specs=vmem,
         compiler_params=params,
         cost_estimate=long(10**6),
-    )(relaxed, ahead)
+    )(both, got)
     value = pl.pallas_call(
         functools.partial(solve_kernel, places),
         out_shape=flat,
@@ -286,7 +266,7 @@
         in_specs=[vmem] * 3,
         out_specs=vmem,
         compiler_params=params,
-    )(turn, exchanged(value), relaxed)
+    )(turn, exchanged(value), got)
     return (corrected, residual)
 
 

time: 61.1 us -> 60.2 us (0.985)
  blocking collectives: 0 us -> 5.44 us
  starting transfers between devices: 45.3 us -> 40.1 us
  Pallas kernels: 6.1 us -> 4.66 us
    all_gather x0 -> x2, blocking collectives: none -> 5.44 us  [the longest x1 3.35 us: on_device(): lax.all_gather(jnp.where(even, high, low), 'lat', axis_index_groups=pairs)]
    ppermute x3 -> x1, starting transfers between devices: 8.38 us -> 3.1 us  [on_device(): lax.ppermute(passed, 'tm', [(i, (i + 2) % blocks) for i in range(blocks)])]
    pallas_call x2, Pallas kernels: 3.89 us -> 2.44 us  [the longest x1 2.41 us: on_device(): pl.pallas_call(relax_kernel, out_shape=(flat, whole, whole), in_specs=[vm...]
    all_to_all x2, waiting for transfers between devices: 7 us -> 7.8 us  [exchanged(): lax.all_to_all(x.reshape(blocks, -1), 'tm', 0, 0, axis_index_groups=[orde...]
  transfers between devices with their start and end apart: 6 -> 4, of which waited for: 3 -> 2; matrix products, arithmetic and copies ran while one was open for 0% -> 0% of each run, Pallas kernels for 6% -> 3%
where the time goes in v4:
time: 60.2 us; the launch traced here: 59.8 us
  starting transfers between devices  40.1 us (67%)
  waiting for transfers between devices  7.8 us (13%)
  blocking collectives  5.44 us (9%)
  Pallas kernels  4.66 us (8%)
  other arithmetic  0.99 us (2%)
  between operations  0.77 us (1%)
    all_to_all x2, starting transfers between devices, exchanged(): lax.all_to_all(x.reshape(blocks, -1), 'tm', 0, 0, axis_index_groups=[orde...  30.7 us
    all_to_all x2, waiting for transfers between devices, exchanged(): lax.all_to_all(x.reshape(blocks, -1), 'tm', 0, 0, axis_index_groups=[orde...  7.8 us
    ppermute x1, starting transfers between devices, on_device(): second = lax.ppermute(jnp.where(even, low, high), 'lat', outer)  6.36 us
    all_gather x1, blocking collectives, on_device(): lax.all_gather(jnp.where(even, high, low), 'lat', axis_index_groups=pairs)  3.35 us
    ppermute x1, starting transfers between devices, on_device(): lax.ppermute(passed, 'tm', [(i, (i + 2) % blocks) for i in range(blocks)])  3.1 us
    pallas_call x1, Pallas kernels, on_device(): pl.pallas_call(relax_kernel, out_shape=(flat, whole, whole), in_specs=[vm...  2.41 us
    all_gather x1, blocking collectives, on_device(): lax.all_gather(relaxed, 'tm', axis_index_groups=[[i, i + 1] for i in rang...  2.09 us
  transfers between devices with their start and end apart: 4, of which 2 were waited for; matrix products, arithmetic and copies ran while one was open for 0% of the time, Pallas kernels for 3%

profile of v4, /device:TPU:1, one launch (start us, length us, event | category | flops | bytes accessed | tf_op | source)
XLA Modules:
  0.0 59.8 jit_solution(13584272141120915657)
XLA Ops:
  0.6 1.0 %bitcast_select_fusion.state_ref = f32[3,64,256]{2,1,0:T(8,128)S(1)} fusion(f32[3,64,256]{2,1,0:T(8,128)} %param.5, f32[1,3,64,256]{3,2,1,0:T(8,128)} %param.4, pred[]{:T(512)S(6)} %eq.12), kind=kLoop, calls=%fused_computation | loop fusion | flops 49152 | bytes 589825 | tf_op jit(solution)/shard_map/jit(_where)/select_n | solution.py:215
  1.6 0.0 copy-start
  1.6 0.0 copy-start.1
  1.6 6.4 %collective-permute-start = (f32[3,8,256]{2,1,0:T(8,128)S(1)}, f32[3,8,256]{2,1,0:T(8,128)S(1)}, u32[]{:S(2)}, u32[]{:S(2)}) collective-permute-start(f32[3,8,256]{2,1,0:T(8,128)S(1)} %get-tuple-element.9), channel_id=1, source_target_pairs={{0,7},{1,2},{2,1},{3,4},{4,3},{5,6},{6,5},{7,0},{8,15},{9,10},{10,... | collective-permute-start | bytes 73736 | tf_op jit(solution)/shard_map/ppermute | solution.py:219
  8.0 3.4 %all-gather = f32[6,8,256]{2,1,0:T(8,128)S(1)} all-gather(f32[3,8,256]{2,1,0:T(8,128)S(1)} %get-tuple-element.8), channel_id=2, replica_groups={{0,1},{2,3},{4,5},{6,7},{8,9},{10,11},{12,13},{14,15},{16,17},{18,19},{..., dimensions={0}, use_global_device_ids=true | all-gather | bytes 73728 | tf_op jit(solution)/shard_map/all_gather | solution.py:221
  11.4 0.0 collective-permute-done.second_ref
  11.4 0.0 copy-done
  11.4 0.0 copy-done.1
  11.4 2.4 %shard_map.59 = (f32[384,128]{1,0:T(8,128)}, f32[3,64,256]{2,1,0:T(8,128)S(1)}, f32[3,64,256]{2,1,0:T(8,128)S(1)}) custom-call(f32[128,128]{1,0:T(8,128)S(1)} %copy-done.1, f32[3,64,256]{2,1,0:T(8,128)S(1)} %bitcast_select_fusion.state_ref, f32[3,8,256]{2,1,0:T(8,128)S(1)} %collective-permute-done.second_ref, f32[2,3,8,256]{3,2,1,0:T(8,128)S(1)} %bitcast.19, ...), custom_call_target="tpu_custom_call" | custom-call | tf_op jit(solution)/shard_map/pallas_call | solution.py:229
  13.8 19.2 %all-to-all-start = ((f32[64,1,768]{2,1,0:T(1,128)}), f32[64,1,768]{2,1,0:T(1,128)S(1)}, u32[]{:S(2)}, u32[]{:S(2)}) async-start(f32[64,1,768]{2,1,0:T(1,128)} %bitcast.7), calls=%async_computation | async-start | bytes 393216 | tf_op jit(solution)/shard_map/all_to_all | solution.py:208
  33.0 2.1 %all-gather.1 = f32[6,64,256]{2,1,0:T(8,128)S(1)} all-gather(f32[3,64,256]{2,1,0:T(8,128)S(1)} %get-tuple-element.6), channel_id=3, replica_groups={{0,8},{16,24},{32,40},{48,56},{64,72},{80,88},{96,104},{112,120},{128,1..., dimensions={0}, use_global_device_ids=true | all-gather | bytes 589824 | tf_op jit(solution)/shard_map/all_gather | solution.py:238
  35.1 3.1 %collective-permute-start.1 = (f32[3,64,256]{2,1,0:T(8,128)S(1)}, f32[3,64,256]{2,1,0:T(8,128)S(1)}, u32[]{:S(2)}, u32[]{:S(2)}) collective-permute-start(f32[3,64,256]{2,1,0:T(8,128)S(1)} %shard_map.61), channel_id=1, source_target_pairs={{0,16},{8,24},{16,32},{24,40},{32,48},{40,56},{48,64},{56,72},{64,... | collective-permute-start | bytes 589832 | tf_op jit(solution)/shard_map/ppermute | solution.py:246
  38.3 1.6 %all-to-all-done = f32[64,1,768]{2,1,0:T(1,128)S(1)} async-done(((f32[64,1,768]{2,1,0:T(1,128)}), f32[64,1,768]{2,1,0:T(1,128)S(1)}, u32[]{:S(2)}, u32[]{:S(2)}) %all-to-all-start) | async-done | bytes 196640 | tf_op jit(solution)/shard_map/all_to_all | solution.py:208
  39.9 0.8 %shard_map.60 = f32[384,128]{1,0:T(8,128)} custom-call(f32[6,128]{1,0:T(8,128)S(1)} %fusion.decay_ref, f32[384,128]{1,0:T(8,128)S(1)} %bitcast.15), custom_call_target="tpu_custom_call" | custom-call | tf_op jit(solution)/shard_map/pallas_call | solution.py:255
  40.7 11.5 %all-to-all-start.1 = ((f32[64,1,768]{2,1,0:T(1,128)}), f32[64,1,768]{2,1,0:T(1,128)S(1)}, u32[]{:S(2)}, u32[]{:S(2)}) async-start(f32[64,1,768]{2,1,0:T(1,128)} %bitcast.9), calls=%async_computation.1 | async-start | bytes 393216 | tf_op jit(solution)/shard_map/all_to_all | solution.py:208
  52.2 0.0 collective-permute-done.1.got_ref
  52.2 0.7 %shard_map.63 = f32[1,3,64,256]{3,2,1,0:T(8,128)} custom-call(f32[2,3,64,256]{3,2,1,0:T(8,128)S(1)} %bitcast.14, f32[3,64,256]{2,1,0:T(8,128)S(1)} %collective-permute-done.1.got_ref), custom_call_target="tpu_custom_call" | custom-call | flops 49152000000 | bytes 393216 | tf_op jit(solution)/shard_map/pallas_call | solution.py:247
  52.9 6.2 %all-to-all-done.1 = f32[64,1,768]{2,1,0:T(1,128)S(1)} async-done(((f32[64,1,768]{2,1,0:T(1,128)}), f32[64,1,768]{2,1,0:T(1,128)S(1)}, u32[]{:S(2)}, u32[]{:S(2)}) %all-to-all-start.1) | async-done | bytes 196640 | tf_op jit(solution)/shard_map/all_to_all | solution.py:208
  59.1 0.7 %shard_map.62 = f32[1,3,64,256]{3,2,1,0:T(8,128)} custom-call(f32[128,128]{1,0:T(8,128)S(1)} %copy-done.1, f32[384,128]{1,0:T(8,128)S(1)} %bitcast.16, f32[3,64,256]{2,1,0:T(8,128)S(1)} %collective-permute-done.1.got_ref), custom_call_target="tpu_custom_call" | custom-call | tf_op jit(solution)/shard_map/pallas_call | solution.py:263
  (4 shorter events, 0.1 us)
Async XLA Ops:
  1.6 9.8 %copy-start = (f32[64,256]{1,0:T(8,128)S(1)}, f32[64,256]{1,0:T(8,128)}, u32[]{:S(2)}) copy-start(f32[64,256]{1,0:T(8,128)} %decay_ref.1) | copy-start | bytes 196612
  1.6 9.8 %copy-start.1 = (f32[128,128]{1,0:T(8,128)S(1)}, f32[128,128]{1,0:T(8,128)}, u32[]{:S(2)}) copy-start(f32[128,128]{1,0:T(8,128)} %constant.38.clone.turn_ref) | copy-start | bytes 196612
  1.6 9.7 %collective-permute-start = (f32[3,8,256]{2,1,0:T(8,128)S(1)}, f32[3,8,256]{2,1,0:T(8,128)S(1)}, u32[]{:S(2)}, u32[]{:S(2)}) collective-permute-start(f32[3,8,256]{2,1,0:T(8,128)S(1)} %get-tuple-element.9), channel_id=1, source_target_pairs={{0,7},{1,2},{2,1},{3,4},{4,3},{5,6},{6,5},{7,0},{8,15},{9,10},{10,... | collective-permute-start | bytes 73736 | tf_op jit(solution)/shard_map/ppermute | solution.py:219
  13.8 26.1 %all-to-all-start = ((f32[64,1,768]{2,1,0:T(1,128)}), f32[64,1,768]{2,1,0:T(1,128)S(1)}, u32[]{:S(2)}, u32[]{:S(2)}) async-start(f32[64,1,768]{2,1,0:T(1,128)} %bitcast.7), calls=%async_computation | async-start | bytes 393216 | tf_op jit(solution)/shard_map/all_to_all | solution.py:208
  35.1 17.0 %collective-permute-start.1 = (f32[3,64,256]{2,1,0:T(8,128)S(1)}, f32[3,64,256]{2,1,0:T(8,128)S(1)}, u32[]{:S(2)}, u32[]{:S(2)}) collective-permute-start(f32[3,64,256]{2,1,0:T(8,128)S(1)} %shard_map.61), channel_id=1, source_target_pairs={{0,16},{8,24},{16,32},{24,40},{32,48},{40,56},{48,64},{56,72},{64,... | collective-permute-start | bytes 589832 | tf_op jit(solution)/shard_map/ppermute | solution.py:246
  40.7 18.4 %all-to-all-start.1 = ((f32[64,1,768]{2,1,0:T(1,128)}), f32[64,1,768]{2,1,0:T(1,128)S(1)}, u32[]{:S(2)}, u32[]{:S(2)}) async-start(f32[64,1,768]{2,1,0:T(1,128)} %bitcast.9), calls=%async_computation.1 | async-start | bytes 393216 | tf_op jit(solution)/shard_map/all_to_all | solution.py:208

commit v5 on v4

--- a/solution.py
+++ b/solution.py
@@ -200,7 +200,7 @@
     whole, flat = f32((planes, rows, lons)), f32((size // LANES, LANES))
     params = pltpu.CompilerParams(vmem_limit_bytes=32 << 20)
     turn = jnp.asarray(turns(blocks))
-    lead = 11 * blocks // 16
+    lead = 45 * blocks // 64
     order = [lead] + [block for block in range(blocks) if block != lead]
     places = [order.index(block) for block in range(blocks)]
 

time: 60.2 us -> 59.3 us (0.985)
  no operation moved by 1% of the time
where the time goes in v5:
time: 59.3 us; the launch traced here: 58.9 us
  starting transfers between devices  39.6 us (67%)
  waiting for transfers between devices  7.47 us (13%)
  blocking collectives  5.44 us (9%)
  Pallas kernels  4.66 us (8%)
  other arithmetic  0.99 us (2%)
  between operations  0.77 us (1%)
    all_to_all x2, starting transfers between devices, exchanged(): lax.all_to_all(x.reshape(blocks, -1), 'tm', 0, 0, axis_index_groups=[orde...  30.1 us
    all_to_all x2, waiting for transfers between devices, exchanged(): lax.all_to_all(x.reshape(blocks, -1), 'tm', 0, 0, axis_index_groups=[orde...  7.47 us
    ppermute x1, starting transfers between devices, on_device(): second = lax.ppermute(jnp.where(even, low, high), 'lat', outer)  6.36 us
    all_gather x1, blocking collectives, on_device(): lax.all_gather(jnp.where(even, high, low), 'lat', axis_index_groups=pairs)  3.35 us
    ppermute x1, starting transfers between devices, on_device(): lax.ppermute(passed, 'tm', [(i, (i + 2) % blocks) for i in range(blocks)])  3.09 us
    pallas_call x1, Pallas kernels, on_device(): pl.pallas_call(relax_kernel, out_shape=(flat, whole, whole), in_specs=[vm...  2.41 us
    all_gather x1, blocking collectives, on_device(): lax.all_gather(relaxed, 'tm', axis_index_groups=[[i, i + 1] for i in rang...  2.09 us
  transfers between devices with their start and end apart: 4, of which 2 were waited for; matrix products, arithmetic and copies ran while one was open for 0% of the time, Pallas kernels for 3%

profile of v5, /device:TPU:1, one launch (start us, length us, event | category | flops | bytes accessed | tf_op | source)
XLA Modules:
  0.0 58.9 jit_solution(14382144394021002748)
XLA Ops:
  0.6 1.0 %bitcast_select_fusion.state_ref = f32[3,64,256]{2,1,0:T(8,128)S(1)} fusion(f32[3,64,256]{2,1,0:T(8,128)} %param.5, f32[1,3,64,256]{3,2,1,0:T(8,128)} %param.4, pred[]{:T(512)S(6)} %eq.12), kind=kLoop, calls=%fused_computation | loop fusion | flops 49152 | bytes 589825 | tf_op jit(solution)/shard_map/jit(_where)/select_n | solution.py:215
  1.6 0.0 copy-start
  1.6 0.0 copy-start.1
  1.6 6.4 %collective-permute-start = (f32[3,8,256]{2,1,0:T(8,128)S(1)}, f32[3,8,256]{2,1,0:T(8,128)S(1)}, u32[]{:S(2)}, u32[]{:S(2)}) collective-permute-start(f32[3,8,256]{2,1,0:T(8,128)S(1)} %get-tuple-element.9), channel_id=1, source_target_pairs={{0,7},{1,2},{2,1},{3,4},{4,3},{5,6},{6,5},{7,0},{8,15},{9,10},{10,... | collective-permute-start | bytes 73736 | tf_op jit(solution)/shard_map/ppermute | solution.py:219
  8.0 3.4 %all-gather = f32[6,8,256]{2,1,0:T(8,128)S(1)} all-gather(f32[3,8,256]{2,1,0:T(8,128)S(1)} %get-tuple-element.8), channel_id=2, replica_groups={{0,1},{2,3},{4,5},{6,7},{8,9},{10,11},{12,13},{14,15},{16,17},{18,19},{..., dimensions={0}, use_global_device_ids=true | all-gather | bytes 73728 | tf_op jit(solution)/shard_map/all_gather | solution.py:221
  11.4 0.0 collective-permute-done.second_ref
  11.4 0.0 copy-done
  11.4 0.0 copy-done.1
  11.4 2.4 %shard_map.59 = (f32[384,128]{1,0:T(8,128)}, f32[3,64,256]{2,1,0:T(8,128)S(1)}, f32[3,64,256]{2,1,0:T(8,128)S(1)}) custom-call(f32[128,128]{1,0:T(8,128)S(1)} %copy-done.1, f32[3,64,256]{2,1,0:T(8,128)S(1)} %bitcast_select_fusion.state_ref, f32[3,8,256]{2,1,0:T(8,128)S(1)} %collective-permute-done.second_ref, f32[2,3,8,256]{3,2,1,0:T(8,128)S(1)} %bitcast.19, ...), custom_call_target="tpu_custom_call" | custom-call | tf_op jit(solution)/shard_map/pallas_call | solution.py:229
  13.8 18.8 %all-to-all-start = ((f32[64,1,768]{2,1,0:T(1,128)}), f32[64,1,768]{2,1,0:T(1,128)S(1)}, u32[]{:S(2)}, u32[]{:S(2)}) async-start(f32[64,1,768]{2,1,0:T(1,128)} %bitcast.7), calls=%async_computation | async-start | bytes 393216 | tf_op jit(solution)/shard_map/all_to_all | solution.py:208
  32.6 2.1 %all-gather.1 = f32[6,64,256]{2,1,0:T(8,128)S(1)} all-gather(f32[3,64,256]{2,1,0:T(8,128)S(1)} %get-tuple-element.6), channel_id=3, replica_groups={{0,8},{16,24},{32,40},{48,56},{64,72},{80,88},{96,104},{112,120},{128,1..., dimensions={0}, use_global_device_ids=true | all-gather | bytes 589824 | tf_op jit(solution)/shard_map/all_gather | solution.py:238
  34.8 3.1 %collective-permute-start.1 = (f32[3,64,256]{2,1,0:T(8,128)S(1)}, f32[3,64,256]{2,1,0:T(8,128)S(1)}, u32[]{:S(2)}, u32[]{:S(2)}) collective-permute-start(f32[3,64,256]{2,1,0:T(8,128)S(1)} %shard_map.61), channel_id=1, source_target_pairs={{0,16},{8,24},{16,32},{24,40},{32,48},{40,56},{48,64},{56,72},{64,... | collective-permute-start | bytes 589832 | tf_op jit(solution)/shard_map/ppermute | solution.py:246
  37.9 1.4 %all-to-all-done = f32[64,1,768]{2,1,0:T(1,128)S(1)} async-done(((f32[64,1,768]{2,1,0:T(1,128)}), f32[64,1,768]{2,1,0:T(1,128)S(1)}, u32[]{:S(2)}, u32[]{:S(2)}) %all-to-all-start) | async-done | bytes 196640 | tf_op jit(solution)/shard_map/all_to_all | solution.py:208
  39.4 0.8 %shard_map.60 = f32[384,128]{1,0:T(8,128)} custom-call(f32[6,128]{1,0:T(8,128)S(1)} %fusion.decay_ref, f32[384,128]{1,0:T(8,128)S(1)} %bitcast.15), custom_call_target="tpu_custom_call" | custom-call | tf_op jit(solution)/shard_map/pallas_call | solution.py:255
  40.2 11.3 %all-to-all-start.1 = ((f32[64,1,768]{2,1,0:T(1,128)}), f32[64,1,768]{2,1,0:T(1,128)S(1)}, u32[]{:S(2)}, u32[]{:S(2)}) async-start(f32[64,1,768]{2,1,0:T(1,128)} %bitcast.9), calls=%async_computation.1 | async-start | bytes 393216 | tf_op jit(solution)/shard_map/all_to_all | solution.py:208
  51.4 0.0 collective-permute-done.1.got_ref
  51.5 0.7 %shard_map.63 = f32[1,3,64,256]{3,2,1,0:T(8,128)} custom-call(f32[2,3,64,256]{3,2,1,0:T(8,128)S(1)} %bitcast.14, f32[3,64,256]{2,1,0:T(8,128)S(1)} %collective-permute-done.1.got_ref), custom_call_target="tpu_custom_call" | custom-call | flops 49152000000 | bytes 393216 | tf_op jit(solution)/shard_map/pallas_call | solution.py:247
  52.2 6.0 %all-to-all-done.1 = f32[64,1,768]{2,1,0:T(1,128)S(1)} async-done(((f32[64,1,768]{2,1,0:T(1,128)}), f32[64,1,768]{2,1,0:T(1,128)S(1)}, u32[]{:S(2)}, u32[]{:S(2)}) %all-to-all-start.1) | async-done | bytes 196640 | tf_op jit(solution)/shard_map/all_to_all | solution.py:208
  58.2 0.7 %shard_map.62 = f32[1,3,64,256]{3,2,1,0:T(8,128)} custom-call(f32[128,128]{1,0:T(8,128)S(1)} %copy-done.1, f32[384,128]{1,0:T(8,128)S(1)} %bitcast.16, f32[3,64,256]{2,1,0:T(8,128)S(1)} %collective-permute-done.1.got_ref), custom_call_target="tpu_custom_call" | custom-call | tf_op jit(solution)/shard_map/pallas_call | solution.py:263
  (4 shorter events, 0.1 us)
Async XLA Ops:
  1.6 9.8 %copy-start = (f32[64,256]{1,0:T(8,128)S(1)}, f32[64,256]{1,0:T(8,128)}, u32[]{:S(2)}) copy-start(f32[64,256]{1,0:T(8,128)} %decay_ref.1) | copy-start | bytes 196612
  1.6 9.8 %copy-start.1 = (f32[128,128]{1,0:T(8,128)S(1)}, f32[128,128]{1,0:T(8,128)}, u32[]{:S(2)}) copy-start(f32[128,128]{1,0:T(8,128)} %constant.38.clone.turn_ref) | copy-start | bytes 196612
  1.6 9.7 %collective-permute-start = (f32[3,8,256]{2,1,0:T(8,128)S(1)}, f32[3,8,256]{2,1,0:T(8,128)S(1)}, u32[]{:S(2)}, u32[]{:S(2)}) collective-permute-start(f32[3,8,256]{2,1,0:T(8,128)S(1)} %get-tuple-element.9), channel_id=1, source_target_pairs={{0,7},{1,2},{2,1},{3,4},{4,3},{5,6},{6,5},{7,0},{8,15},{9,10},{10,... | collective-permute-start | bytes 73736 | tf_op jit(solution)/shard_map/ppermute | solution.py:219
  13.8 25.6 %all-to-all-start = ((f32[64,1,768]{2,1,0:T(1,128)}), f32[64,1,768]{2,1,0:T(1,128)S(1)}, u32[]{:S(2)}, u32[]{:S(2)}) async-start(f32[64,1,768]{2,1,0:T(1,128)} %bitcast.7), calls=%async_computation | async-start | bytes 393216 | tf_op jit(solution)/shard_map/all_to_all | solution.py:208
  34.8 16.7 %collective-permute-start.1 = (f32[3,64,256]{2,1,0:T(8,128)S(1)}, f32[3,64,256]{2,1,0:T(8,128)S(1)}, u32[]{:S(2)}, u32[]{:S(2)}) collective-permute-start(f32[3,64,256]{2,1,0:T(8,128)S(1)} %shard_map.61), channel_id=1, source_target_pairs={{0,16},{8,24},{16,32},{24,40},{32,48},{40,56},{48,64},{56,72},{64,... | collective-permute-start | bytes 589832 | tf_op jit(solution)/shard_map/ppermute | solution.py:246
  40.2 18.0 %all-to-all-start.1 = ((f32[64,1,768]{2,1,0:T(1,128)}), f32[64,1,768]{2,1,0:T(1,128)S(1)}, u32[]{:S(2)}, u32[]{:S(2)}) async-start(f32[64,1,768]{2,1,0:T(1,128)} %bitcast.9), calls=%async_computation.1 | async-start | bytes 393216 | tf_op jit(solution)/shard_map/all_to_all | solution.py:208

commit v6 on v5

--- a/solution.py
+++ b/solution.py
@@ -94,14 +94,14 @@
 
 
 def relax_kernel(
-    turn_ref, state_ref, second_ref, pair_ref, decay_ref, term_ref, relaxed_ref, ahead_ref, term, sem
+    turn_ref, state_ref, first_ref, pair_ref, decay_ref, term_ref, relaxed_ref, ahead_ref, term, sem
 ):
     even = lax.rem(lax.axis_index("lat"), 2) == 0
     rows, lons = state_ref.shape[1:]
     state = []
     for plane in range(3):
-        first = jnp.where(even, pair_ref[1, plane], pair_ref[0, plane])
-        second = second_ref[plane]
+        first = first_ref[plane]
+        second = jnp.where(even, pair_ref[0, plane], pair_ref[1, plane])
         below = jnp.where(even, second, first)
         above = jnp.where(even, first, second)
         state.append(jnp.concatenate([below, state_ref[plane], above], axis=0))
@@ -215,10 +215,10 @@
     state = jnp.where(mine == blocks - 1, initial_state, states[0])
     even = slab % 2 == 0
     low, high = state[:, :HALO], state[:, -HALO:]
-    outer = [(i, (i - 1 if i % 2 == 0 else i + 1) % slabs) for i in range(slabs)]
-    second = lax.ppermute(jnp.where(even, low, high), "lat", outer)
-    pairs = [[i, i + 1] for i in range(0, slabs, 2)]
-    pair = lax.all_gather(jnp.where(even, high, low), "lat", axis_index_groups=pairs)
+    inner = [(i, i ^ 1) for i in range(slabs)]
+    first = lax.ppermute(jnp.where(even, high, low), "lat", inner)
+    pairs = [[i, (i + 1) % slabs] for i in range(1, slabs, 2)]
+    pair = lax.all_gather(jnp.where(even, low, high), "lat", axis_index_groups=pairs)
 
     tiles = coarse_decay.reshape(rows // 8, 8, lons // LANES, LANES).transpose(0, 2, 1, 3)
     tiles = tiles.reshape(-1, LANES)
@@ -233,7 +233,7 @@
         out_specs=(hbm, vmem, vmem),
         scratch_shapes=[pltpu.VMEM(flat.shape, jnp.float32), pltpu.SemaphoreType.DMA((1,))],
         compiler_params=params,
-    )(turn, state, second, pair, coarse_decay)
+    )(turn, state, first, pair, coarse_decay)
 
     both = lax.all_gather(relaxed, "tm", axis_index_groups=[[i, i + 1] for i in range(0, blocks, 2)])
     passed = pl.pallas_call(

time: 59.3 us -> 59.1 us (level)
  starting transfers between devices: 39.6 us -> 37.2 us
  blocking collectives: 5.44 us -> 7.55 us
    ppermute x1, starting transfers between devices: 6.36 us -> 4.17 us  [on_device(): first = lax.ppermute(jnp.where(even, high, low), 'lat', inner)]
    all_gather x1, blocking collectives: 3.35 us -> 5.46 us  [on_device(): lax.all_gather(jnp.where(even, low, high), 'lat', axis_index_groups=pairs)]
where the time goes in v6:
time: 59.1 us; the launch traced here: 58.7 us
  starting transfers between devices  37.2 us (63%)
  waiting for transfers between devices  7.57 us (13%)
  blocking collectives  7.55 us (13%)
  Pallas kernels  4.66 us (8%)
  other arithmetic  0.99 us (2%)
  between operations  0.77 us (1%)
    all_to_all x2, starting transfers between devices, exchanged(): lax.all_to_all(x.reshape(blocks, -1), 'tm', 0, 0, axis_index_groups=[orde...  29.9 us
    all_to_all x2, waiting for transfers between devices, exchanged(): lax.all_to_all(x.reshape(blocks, -1), 'tm', 0, 0, axis_index_groups=[orde...  7.56 us
    all_gather x1, blocking collectives, on_device(): lax.all_gather(jnp.where(even, low, high), 'lat', axis_index_groups=pairs)  5.46 us
    ppermute x1, starting transfers between devices, on_device(): first = lax.ppermute(jnp.where(even, high, low), 'lat', inner)  4.17 us
    ppermute x1, starting transfers between devices, on_device(): lax.ppermute(passed, 'tm', [(i, (i + 2) % blocks) for i in range(blocks)])  3.09 us
    pallas_call x1, Pallas kernels, on_device(): pl.pallas_call(relax_kernel, out_shape=(flat, whole, whole), in_specs=[vm...  2.41 us
    all_gather x1, blocking collectives, on_device(): lax.all_gather(relaxed, 'tm', axis_index_groups=[[i, i + 1] for i in rang...  2.09 us
  transfers between devices with their start and end apart: 4, of which 2 were waited for; matrix products, arithmetic and copies ran while one was open for 0% of the time, Pallas kernels for 3%

profile of v6, /device:TPU:1, one launch (start us, length us, event | category | flops | bytes accessed | tf_op | source)
XLA Modules:
  0.0 58.7 jit_solution(2697962234330996774)
XLA Ops:
  0.6 1.0 %bitcast_select_fusion.state_ref = f32[3,64,256]{2,1,0:T(8,128)S(1)} fusion(f32[3,64,256]{2,1,0:T(8,128)} %param.5, f32[1,3,64,256]{3,2,1,0:T(8,128)} %param.4, pred[]{:T(512)S(6)} %eq.12), kind=kLoop, calls=%fused_computation | loop fusion | flops 49152 | bytes 589825 | tf_op jit(solution)/shard_map/jit(_where)/select_n | solution.py:215
  1.6 0.0 copy-start
  1.6 0.0 copy-start.1
  1.6 4.2 %collective-permute-start = (f32[3,8,256]{2,1,0:T(8,128)S(1)}, f32[3,8,256]{2,1,0:T(8,128)S(1)}, u32[]{:S(2)}, u32[]{:S(2)}) collective-permute-start(f32[3,8,256]{2,1,0:T(8,128)S(1)} %get-tuple-element.9), channel_id=1, source_target_pairs={{0,1},{1,0},{2,3},{3,2},{4,5},{5,4},{6,7},{7,6},{8,9},{9,8},{10,11... | collective-permute-start | bytes 73736 | tf_op jit(solution)/shard_map/ppermute | solution.py:219
  5.8 5.5 %all-gather = f32[6,8,256]{2,1,0:T(8,128)S(1)} all-gather(f32[3,8,256]{2,1,0:T(8,128)S(1)} %get-tuple-element.8), channel_id=2, replica_groups={{1,2},{3,4},{5,6},{7,0},{9,10},{11,12},{13,14},{15,8},{17,18},{19,20},{..., dimensions={0}, use_global_device_ids=true | all-gather | bytes 73728 | tf_op jit(solution)/shard_map/all_gather | solution.py:221
  11.3 0.0 collective-permute-done.first_ref
  11.3 0.0 copy-done
  11.3 0.0 copy-done.1
  11.3 2.4 %shard_map.59 = (f32[384,128]{1,0:T(8,128)}, f32[3,64,256]{2,1,0:T(8,128)S(1)}, f32[3,64,256]{2,1,0:T(8,128)S(1)}) custom-call(f32[128,128]{1,0:T(8,128)S(1)} %copy-done.1, f32[3,64,256]{2,1,0:T(8,128)S(1)} %bitcast_select_fusion.state_ref, f32[3,8,256]{2,1,0:T(8,128)S(1)} %collective-permute-done.first_ref, f32[2,3,8,256]{3,2,1,0:T(8,128)S(1)} %bitcast.19, ...), custom_call_target="tpu_custom_call" | custom-call | tf_op jit(solution)/shard_map/pallas_call | solution.py:229
  13.7 18.8 %all-to-all-start = ((f32[64,1,768]{2,1,0:T(1,128)}), f32[64,1,768]{2,1,0:T(1,128)S(1)}, u32[]{:S(2)}, u32[]{:S(2)}) async-start(f32[64,1,768]{2,1,0:T(1,128)} %bitcast.7), calls=%async_computation | async-start | bytes 393216 | tf_op jit(solution)/shard_map/all_to_all | solution.py:208
  32.6 2.1 %all-gather.1 = f32[6,64,256]{2,1,0:T(8,128)S(1)} all-gather(f32[3,64,256]{2,1,0:T(8,128)S(1)} %get-tuple-element.6), channel_id=3, replica_groups={{0,8},{16,24},{32,40},{48,56},{64,72},{80,88},{96,104},{112,120},{128,1..., dimensions={0}, use_global_device_ids=true | all-gather | bytes 589824 | tf_op jit(solution)/shard_map/all_gather | solution.py:238
  34.7 3.1 %collective-permute-start.1 = (f32[3,64,256]{2,1,0:T(8,128)S(1)}, f32[3,64,256]{2,1,0:T(8,128)S(1)}, u32[]{:S(2)}, u32[]{:S(2)}) collective-permute-start(f32[3,64,256]{2,1,0:T(8,128)S(1)} %shard_map.61), channel_id=1, source_target_pairs={{0,16},{8,24},{16,32},{24,40},{32,48},{40,56},{48,64},{56,72},{64,... | collective-permute-start | bytes 589832 | tf_op jit(solution)/shard_map/ppermute | solution.py:246
  37.8 1.6 %all-to-all-done = f32[64,1,768]{2,1,0:T(1,128)S(1)} async-done(((f32[64,1,768]{2,1,0:T(1,128)}), f32[64,1,768]{2,1,0:T(1,128)S(1)}, u32[]{:S(2)}, u32[]{:S(2)}) %all-to-all-start) | async-done | bytes 196640 | tf_op jit(solution)/shard_map/all_to_all | solution.py:208
  39.5 0.8 %shard_map.60 = f32[384,128]{1,0:T(8,128)} custom-call(f32[6,128]{1,0:T(8,128)S(1)} %fusion.decay_ref, f32[384,128]{1,0:T(8,128)S(1)} %bitcast.15), custom_call_target="tpu_custom_call" | custom-call | tf_op jit(solution)/shard_map/pallas_call | solution.py:255
  40.3 11.1 %all-to-all-start.1 = ((f32[64,1,768]{2,1,0:T(1,128)}), f32[64,1,768]{2,1,0:T(1,128)S(1)}, u32[]{:S(2)}, u32[]{:S(2)}) async-start(f32[64,1,768]{2,1,0:T(1,128)} %bitcast.9), calls=%async_computation.1 | async-start | bytes 393216 | tf_op jit(solution)/shard_map/all_to_all | solution.py:208
  51.4 0.0 collective-permute-done.1.got_ref
  51.4 0.7 %shard_map.63 = f32[1,3,64,256]{3,2,1,0:T(8,128)} custom-call(f32[2,3,64,256]{3,2,1,0:T(8,128)S(1)} %bitcast.14, f32[3,64,256]{2,1,0:T(8,128)S(1)} %collective-permute-done.1.got_ref), custom_call_target="tpu_custom_call" | custom-call | flops 49152000000 | bytes 393216 | tf_op jit(solution)/shard_map/pallas_call | solution.py:247
  52.1 5.9 %all-to-all-done.1 = f32[64,1,768]{2,1,0:T(1,128)S(1)} async-done(((f32[64,1,768]{2,1,0:T(1,128)}), f32[64,1,768]{2,1,0:T(1,128)S(1)}, u32[]{:S(2)}, u32[]{:S(2)}) %all-to-all-start.1) | async-done | bytes 196640 | tf_op jit(solution)/shard_map/all_to_all | solution.py:208
  58.0 0.7 %shard_map.62 = f32[1,3,64,256]{3,2,1,0:T(8,128)} custom-call(f32[128,128]{1,0:T(8,128)S(1)} %copy-done.1, f32[384,128]{1,0:T(8,128)S(1)} %bitcast.16, f32[3,64,256]{2,1,0:T(8,128)S(1)} %collective-permute-done.1.got_ref), custom_call_target="tpu_custom_call" | custom-call | tf_op jit(solution)/shard_map/pallas_call | solution.py:263
  (4 shorter events, 0.1 us)
Async XLA Ops:
  1.6 9.7 %copy-start = (f32[64,256]{1,0:T(8,128)S(1)}, f32[64,256]{1,0:T(8,128)}, u32[]{:S(2)}) copy-start(f32[64,256]{1,0:T(8,128)} %decay_ref.1) | copy-start | bytes 196612
  1.6 9.7 %copy-start.1 = (f32[128,128]{1,0:T(8,128)S(1)}, f32[128,128]{1,0:T(8,128)}, u32[]{:S(2)}) copy-start(f32[128,128]{1,0:T(8,128)} %constant.38.clone.turn_ref) | copy-start | bytes 196612
  1.6 9.6 %collective-permute-start = (f32[3,8,256]{2,1,0:T(8,128)S(1)}, f32[3,8,256]{2,1,0:T(8,128)S(1)}, u32[]{:S(2)}, u32[]{:S(2)}) collective-permute-start(f32[3,8,256]{2,1,0:T(8,128)S(1)} %get-tuple-element.9), channel_id=1, source_target_pairs={{0,1},{1,0},{2,3},{3,2},{4,5},{5,4},{6,7},{7,6},{8,9},{9,8},{10,11... | collective-permute-start | bytes 73736 | tf_op jit(solution)/shard_map/ppermute | solution.py:219
  13.7 25.8 %all-to-all-start = ((f32[64,1,768]{2,1,0:T(1,128)}), f32[64,1,768]{2,1,0:T(1,128)S(1)}, u32[]{:S(2)}, u32[]{:S(2)}) async-start(f32[64,1,768]{2,1,0:T(1,128)} %bitcast.7), calls=%async_computation | async-start | bytes 393216 | tf_op jit(solution)/shard_map/all_to_all | solution.py:208
  34.7 16.7 %collective-permute-start.1 = (f32[3,64,256]{2,1,0:T(8,128)S(1)}, f32[3,64,256]{2,1,0:T(8,128)S(1)}, u32[]{:S(2)}, u32[]{:S(2)}) collective-permute-start(f32[3,64,256]{2,1,0:T(8,128)S(1)} %shard_map.61), channel_id=1, source_target_pairs={{0,16},{8,24},{16,32},{24,40},{32,48},{40,56},{48,64},{56,72},{64,... | collective-permute-start | bytes 589832 | tf_op jit(solution)/shard_map/ppermute | solution.py:246
  40.3 17.7 %all-to-all-start.1 = ((f32[64,1,768]{2,1,0:T(1,128)}), f32[64,1,768]{2,1,0:T(1,128)S(1)}, u32[]{:S(2)}, u32[]{:S(2)}) async-start(f32[64,1,768]{2,1,0:T(1,128)} %bitcast.9), calls=%async_computation.1 | async-start | bytes 393216 | tf_op jit(solution)/shard_map/all_to_all | solution.py:208

commit v7 on v6

--- a/solution.py
+++ b/solution.py
@@ -107,6 +107,7 @@
         state.append(jnp.concatenate([below, state_ref[plane], above], axis=0))
     relaxed, ahead = two_blocks(state)
     per_plane = term.shape[0] // 3
+    copies = []
     for row in range(0, rows, 8):
         for col in range(0, lons, LANES):
             cols = slice(col, col + LANES)
@@ -115,12 +116,19 @@
             to = row * lons // LANES + col * 8 // LANES
             for plane, value in enumerate(forcing(turn_ref, decay_ref[row : row + 8, cols], *tiles)):
                 term[plane * per_plane + to : plane * per_plane + to + 8] = value
-    copy = pltpu.make_async_copy(term, term_ref, sem.at[0])
-    copy.start()
+        if (row + 8) % (rows // 2) == 0:
+            half = per_plane // 2
+            for plane in range(3):
+                part = pl.ds(plane * per_plane + (row + 8) * lons // LANES - half, half)
+                copies.append(
+                    pltpu.make_async_copy(term.at[part], term_ref.at[part], sem.at[len(copies)])
+                )
+                copies[-1].start()
     for to, values in ((relaxed_ref, relaxed), (ahead_ref, ahead)):
         for plane, value in enumerate(values):
             to[plane] = value[HALO : HALO + rows]
-    copy.wait()
+    for copy in copies:
+        copy.wait()
 
 
 def solve_kernel(places, decay_ref, term_ref, value_ref, values, sem):
@@ -231,7 +239,7 @@
         out_shape=(flat, whole, whole),
         in_specs=[vmem] * 5,
         out_specs=(hbm, vmem, vmem),
-        scratch_shapes=[pltpu.VMEM(flat.shape, jnp.float32), pltpu.SemaphoreType.DMA((1,))],
+        scratch_shapes=[pltpu.VMEM(flat.shape, jnp.float32), pltpu.SemaphoreType.DMA((6,))],
         compiler_params=params,
     )(turn, state, first, pair, coarse_decay)
 

time: 59.1 us -> 59.1 us (level)
  no operation moved by 1% of the time
where the time goes in v7:
time: 59.1 us; the launch traced here: 58.7 us
  starting transfers between devices  37.2 us (63%)
  waiting for transfers between devices  7.57 us (13%)
  blocking collectives  7.55 us (13%)
  Pallas kernels  4.66 us (8%)
  other arithmetic  0.99 us (2%)
  between operations  0.77 us (1%)
    all_to_all x2, starting transfers between devices, exchanged(): lax.all_to_all(x.reshape(blocks, -1), 'tm', 0, 0, axis_index_groups=[orde...  29.9 us
    all_to_all x2, waiting for transfers between devices, exchanged(): lax.all_to_all(x.reshape(blocks, -1), 'tm', 0, 0, axis_index_groups=[orde...  7.56 us
    all_gather x1, blocking collectives, on_device(): lax.all_gather(jnp.where(even, low, high), 'lat', axis_index_groups=pairs)  5.46 us
    ppermute x1, starting transfers between devices, on_device(): first = lax.ppermute(jnp.where(even, high, low), 'lat', inner)  4.17 us
    ppermute x1, starting transfers between devices, on_device(): lax.ppermute(passed, 'tm', [(i, (i + 2) % blocks) for i in range(blocks)])  3.09 us
    pallas_call x1, Pallas kernels, on_device(): pl.pallas_call(relax_kernel, out_shape=(flat, whole, whole), in_specs=[vm...  2.41 us
    all_gather x1, blocking collectives, on_device(): lax.all_gather(relaxed, 'tm', axis_index_groups=[[i, i + 1] for i in rang...  2.09 us
  transfers between devices with their start and end apart: 4, of which 2 were waited for; matrix products, arithmetic and copies ran while one was open for 0% of the time, Pallas kernels for 3%

profile of v7, /device:TPU:1, one launch (start us, length us, event | category | flops | bytes accessed | tf_op | source)
XLA Modules:
  0.0 58.7 jit_solution(692068589809086831)
XLA Ops:
  0.6 1.0 %bitcast_select_fusion.state_ref = f32[3,64,256]{2,1,0:T(8,128)S(1)} fusion(f32[3,64,256]{2,1,0:T(8,128)} %param.5, f32[1,3,64,256]{3,2,1,0:T(8,128)} %param.4, pred[]{:T(512)S(6)} %eq.12), kind=kLoop, calls=%fused_computation | loop fusion | flops 49152 | bytes 589825 | tf_op jit(solution)/shard_map/jit(_where)/select_n | solution.py:223
  1.6 0.0 copy-start
  1.6 0.0 copy-start.1
  1.6 4.2 %collective-permute-start = (f32[3,8,256]{2,1,0:T(8,128)S(1)}, f32[3,8,256]{2,1,0:T(8,128)S(1)}, u32[]{:S(2)}, u32[]{:S(2)}) collective-permute-start(f32[3,8,256]{2,1,0:T(8,128)S(1)} %get-tuple-element.9), channel_id=1, source_target_pairs={{0,1},{1,0},{2,3},{3,2},{4,5},{5,4},{6,7},{7,6},{8,9},{9,8},{10,11... | collective-permute-start | bytes 73736 | tf_op jit(solution)/shard_map/ppermute | solution.py:227
  5.8 5.5 %all-gather = f32[6,8,256]{2,1,0:T(8,128)S(1)} all-gather(f32[3,8,256]{2,1,0:T(8,128)S(1)} %get-tuple-element.8), channel_id=2, replica_groups={{1,2},{3,4},{5,6},{7,0},{9,10},{11,12},{13,14},{15,8},{17,18},{19,20},{..., dimensions={0}, use_global_device_ids=true | all-gather | bytes 73728 | tf_op jit(solution)/shard_map/all_gather | solution.py:229
  11.3 0.0 collective-permute-done.first_ref
  11.3 0.0 copy-done
  11.3 0.0 copy-done.1
  11.3 2.4 %shard_map.59 = (f32[384,128]{1,0:T(8,128)}, f32[3,64,256]{2,1,0:T(8,128)S(1)}, f32[3,64,256]{2,1,0:T(8,128)S(1)}) custom-call(f32[128,128]{1,0:T(8,128)S(1)} %copy-done.1, f32[3,64,256]{2,1,0:T(8,128)S(1)} %bitcast_select_fusion.state_ref, f32[3,8,256]{2,1,0:T(8,128)S(1)} %collective-permute-done.first_ref, f32[2,3,8,256]{3,2,1,0:T(8,128)S(1)} %bitcast.19, ...), custom_call_target="tpu_custom_call" | custom-call | tf_op jit(solution)/shard_map/pallas_call | solution.py:237
  13.7 18.8 %all-to-all-start = ((f32[64,1,768]{2,1,0:T(1,128)}), f32[64,1,768]{2,1,0:T(1,128)S(1)}, u32[]{:S(2)}, u32[]{:S(2)}) async-start(f32[64,1,768]{2,1,0:T(1,128)} %bitcast.7), calls=%async_computation | async-start | bytes 393216 | tf_op jit(solution)/shard_map/all_to_all | solution.py:216
  32.6 2.1 %all-gather.1 = f32[6,64,256]{2,1,0:T(8,128)S(1)} all-gather(f32[3,64,256]{2,1,0:T(8,128)S(1)} %get-tuple-element.6), channel_id=3, replica_groups={{0,8},{16,24},{32,40},{48,56},{64,72},{80,88},{96,104},{112,120},{128,1..., dimensions={0}, use_global_device_ids=true | all-gather | bytes 589824 | tf_op jit(solution)/shard_map/all_gather | solution.py:246
  34.7 3.1 %collective-permute-start.1 = (f32[3,64,256]{2,1,0:T(8,128)S(1)}, f32[3,64,256]{2,1,0:T(8,128)S(1)}, u32[]{:S(2)}, u32[]{:S(2)}) collective-permute-start(f32[3,64,256]{2,1,0:T(8,128)S(1)} %shard_map.61), channel_id=1, source_target_pairs={{0,16},{8,24},{16,32},{24,40},{32,48},{40,56},{48,64},{56,72},{64,... | collective-permute-start | bytes 589832 | tf_op jit(solution)/shard_map/ppermute | solution.py:254
  37.9 1.6 %all-to-all-done = f32[64,1,768]{2,1,0:T(1,128)S(1)} async-done(((f32[64,1,768]{2,1,0:T(1,128)}), f32[64,1,768]{2,1,0:T(1,128)S(1)}, u32[]{:S(2)}, u32[]{:S(2)}) %all-to-all-start) | async-done | bytes 196640 | tf_op jit(solution)/shard_map/all_to_all | solution.py:216
  39.5 0.8 %shard_map.60 = f32[384,128]{1,0:T(8,128)} custom-call(f32[6,128]{1,0:T(8,128)S(1)} %fusion.decay_ref, f32[384,128]{1,0:T(8,128)S(1)} %bitcast.15), custom_call_target="tpu_custom_call" | custom-call | tf_op jit(solution)/shard_map/pallas_call | solution.py:263
  40.3 11.1 %all-to-all-start.1 = ((f32[64,1,768]{2,1,0:T(1,128)}), f32[64,1,768]{2,1,0:T(1,128)S(1)}, u32[]{:S(2)}, u32[]{:S(2)}) async-start(f32[64,1,768]{2,1,0:T(1,128)} %bitcast.9), calls=%async_computation.1 | async-start | bytes 393216 | tf_op jit(solution)/shard_map/all_to_all | solution.py:216
  51.4 0.0 collective-permute-done.1.got_ref
  51.4 0.7 %shard_map.63 = f32[1,3,64,256]{3,2,1,0:T(8,128)} custom-call(f32[2,3,64,256]{3,2,1,0:T(8,128)S(1)} %bitcast.14, f32[3,64,256]{2,1,0:T(8,128)S(1)} %collective-permute-done.1.got_ref), custom_call_target="tpu_custom_call" | custom-call | flops 49152000000 | bytes 393216 | tf_op jit(solution)/shard_map/pallas_call | solution.py:255
  52.1 5.9 %all-to-all-done.1 = f32[64,1,768]{2,1,0:T(1,128)S(1)} async-done(((f32[64,1,768]{2,1,0:T(1,128)}), f32[64,1,768]{2,1,0:T(1,128)S(1)}, u32[]{:S(2)}, u32[]{:S(2)}) %all-to-all-start.1) | async-done | bytes 196640 | tf_op jit(solution)/shard_map/all_to_all | solution.py:216
  58.0 0.7 %shard_map.62 = f32[1,3,64,256]{3,2,1,0:T(8,128)} custom-call(f32[128,128]{1,0:T(8,128)S(1)} %copy-done.1, f32[384,128]{1,0:T(8,128)S(1)} %bitcast.16, f32[3,64,256]{2,1,0:T(8,128)S(1)} %collective-permute-done.1.got_ref), custom_call_target="tpu_custom_call" | custom-call | tf_op jit(solution)/shard_map/pallas_call | solution.py:271
  (4 shorter events, 0.1 us)
Async XLA Ops:
  1.6 9.7 %copy-start = (f32[64,256]{1,0:T(8,128)S(1)}, f32[64,256]{1,0:T(8,128)}, u32[]{:S(2)}) copy-start(f32[64,256]{1,0:T(8,128)} %decay_ref.1) | copy-start | bytes 196612
  1.6 9.7 %copy-start.1 = (f32[128,128]{1,0:T(8,128)S(1)}, f32[128,128]{1,0:T(8,128)}, u32[]{:S(2)}) copy-start(f32[128,128]{1,0:T(8,128)} %constant.38.clone.turn_ref) | copy-start | bytes 196612
  1.6 9.6 %collective-permute-start = (f32[3,8,256]{2,1,0:T(8,128)S(1)}, f32[3,8,256]{2,1,0:T(8,128)S(1)}, u32[]{:S(2)}, u32[]{:S(2)}) collective-permute-start(f32[3,8,256]{2,1,0:T(8,128)S(1)} %get-tuple-element.9), channel_id=1, source_target_pairs={{0,1},{1,0},{2,3},{3,2},{4,5},{5,4},{6,7},{7,6},{8,9},{9,8},{10,11... | collective-permute-start | bytes 73736 | tf_op jit(solution)/shard_map/ppermute | solution.py:227
  13.7 25.8 %all-to-all-start = ((f32[64,1,768]{2,1,0:T(1,128)}), f32[64,1,768]{2,1,0:T(1,128)S(1)}, u32[]{:S(2)}, u32[]{:S(2)}) async-start(f32[64,1,768]{2,1,0:T(1,128)} %bitcast.7), calls=%async_computation | async-start | bytes 393216 | tf_op jit(solution)/shard_map/all_to_all | solution.py:216
  34.7 16.7 %collective-permute-start.1 = (f32[3,64,256]{2,1,0:T(8,128)S(1)}, f32[3,64,256]{2,1,0:T(8,128)S(1)}, u32[]{:S(2)}, u32[]{:S(2)}) collective-permute-start(f32[3,64,256]{2,1,0:T(8,128)S(1)} %shard_map.61), channel_id=1, source_target_pairs={{0,16},{8,24},{16,32},{24,40},{32,48},{40,56},{48,64},{56,72},{64,... | collective-permute-start | bytes 589832 | tf_op jit(solution)/shard_map/ppermute | solution.py:254
  40.3 17.7 %all-to-all-start.1 = ((f32[64,1,768]{2,1,0:T(1,128)}), f32[64,1,768]{2,1,0:T(1,128)S(1)}, u32[]{:S(2)}, u32[]{:S(2)}) async-start(f32[64,1,768]{2,1,0:T(1,128)} %bitcast.9), calls=%async_computation.1 | async-start | bytes 393216 | tf_op jit(solution)/shard_map/all_to_all | solution.py:216
